TPU v7x, 32 devices: a whole 2x2x4 slice. The times are simulated.
32 devices in a mesh: comp: 2 (over core), blk: 16 (over z, y, x).
Axes of the slice: x: 2, y: 2, z: 4, core: 2. Of those that a mesh axis runs over, the one named last changes fastest.
Arguments:
- thermal_profiles: float32 [2, 80, 131072], P('comp', None, 'blk'), may hold values from -6 to 6
- adjacent_positions: int32 [2, 6, 131072], P('comp', None, 'blk'), may hold values from 0 to 10239
- diffusion_link_factor: float32 [2, 6, 131072], P('comp', None, 'blk'), may hold values from 0.01 to 0.15
- implicit_solver_matrix: float32 [2, 80, 80], P('comp'), may hold values from -0.6 to 1.2
- lagged_surface_temp: float32 [131072], P('blk'), may hold values from -6 to 6
- flux_coefficient: float32 [16, 131072], P(None, 'blk'), may hold values from 0.2 to 2
- flux_heating: float32 [16], replicated, may hold values from -3 to 3
- ocean_cell_mask: int32 [131072], P('blk'), may hold values 0 or 1
- atmosphere_slot_cells: int32 [16, 16, 256], P('blk'), may hold values from 0 to 8191
- ocean_slot_cells: int32 [16, 16, 512], P('blk'), may hold values from 0 to 8191
- forward_weight_blocks: float32 [16, 16, 512, 256], P('blk'), may hold values from -0.375 to 0.375
- backward_weight_blocks: float32 [16, 16, 256, 512], P('blk'), may hold values from -0.25 to 0.25
Outputs:
- partition_thermal_result: float32 [2, 80, 131072], P('comp', None, 'blk')
- interface_exchange_values: float32 [2, 16, 131072], P('comp', None, 'blk')
- interface_warmth_values: float32 [2, 131072], P('comp', 'blk')
All inputs are finite; a program needn't handle non-finite values. No bound on the sum of `ocean_cell_mask` on one device may be relied on, other than what follows from the above.
Results may differ from a plain program's by a relative error of at most 0.0001.
Values sent between devices are 32-bit elements; how exact they have to be, the bound alone decides.
No kernel may reach another device: no remote copies, remote signals or barrier semaphores. Data moves between devices by JAX's collectives and lax.ppermute only.
A program may use at most 128 MiB of HBM per device.

v0:
```python
import jax
import jax.numpy as jnp
from jax import lax
from jax.sharding import PartitionSpec as P

HALO = 1024


def with_halo(shard, sides, width):
    for axis, dim in sides:
        count, length = (lax.axis_size(axis), shard.shape[dim])
        up = [(i, (i + 1) % count) for i in range(count)]
        down = [(j, i) for i, j in up]
        last = lax.slice_in_dim(shard, length - width, length, axis=dim)
        initial = lax.slice_in_dim(shard, 0, width, axis=dim)
        before = lax.ppermute(last, axis, up)
        after = lax.ppermute(initial, axis, down)
        shard = jnp.concatenate([before, shard, after], axis=dim)
    return shard


def pick_rows(table, where):
    return jnp.take(table, where, axis=0)


def add_rows(values, where, count):
    start = jnp.zeros((count, values.shape[1]), jnp.float32)
    return start.at[where].add(values)


def advance(owner_state, nearby, edge_w, solver):
    extended = with_halo(owner_state, (("blk", 1),), HALO)
    change = jnp.zeros_like(owner_state)
    for j in range(nearby.shape[0]):
        picked = jnp.take(extended, nearby[j], axis=1)
        change = change + edge_w[j][None, :] * (picked - owner_state)
    updated = owner_state + change
    return jnp.dot(solver, updated, precision=lax.Precision.HIGHEST)


def shards(
    thermal_profiles,
    adjacent_positions,
    diffusion_link_factor,
    implicit_solver_matrix,
    lagged_surface_temp,
    flux_coefficient,
    flux_heating,
    ocean_cell_mask,
    atmosphere_slot_cells,
    ocean_slot_cells,
    forward_weight_blocks,
    backward_weight_blocks,
):
    blocks = lax.axis_size("blk")
    ocean_section = lax.axis_index("comp") == 1
    water_indicator = ocean_cell_mask.astype(jnp.float32)
    owner_state = thermal_profiles[0]
    level_stack = owner_state.shape[0]
    flux_count = flux_coefficient.shape[0]
    cell_count = owner_state.shape[1]
    atmosphere_flux = (
        flux_coefficient * (owner_state[level_stack - 1] - lagged_surface_temp)[None, :]
    )
    atm_slot_rows = atmosphere_slot_cells[0]
    slot_atm = atm_slot_rows.shape[1]
    payload = pick_rows(atmosphere_flux.T, atm_slot_rows.reshape(-1)).reshape(
        blocks, slot_atm * flux_count
    )
    padding = jnp.zeros_like(payload)
    outgoing = jnp.concatenate([padding, payload], axis=0)
    incoming = lax.all_to_all(outgoing, ("comp", "blk"), split_axis=0, concat_axis=0, tiled=True)
    arrived = incoming[:blocks]
    arrived_rows = arrived.reshape(blocks, slot_atm, flux_count)
    mapped = jnp.einsum(
        "ajk,akf->ajf", forward_weight_blocks[0], arrived_rows, precision=lax.Precision.HIGHEST
    )
    ocean_slot_row_list = ocean_slot_cells[0]
    slot_ocean = ocean_slot_row_list.shape[1]
    ocean_rows = add_rows(
        mapped.reshape(blocks * slot_ocean, flux_count), ocean_slot_row_list.reshape(-1), cell_count
    )
    ocean_flux = ocean_rows.T * water_indicator[None, :]
    driving_source = jnp.sum(flux_heating[:, None] * ocean_flux, axis=0)
    current_state = owner_state.at[0].add(
        jnp.where(ocean_section, driving_source, jnp.zeros_like(driving_source))
    )
    for step in range(2):
        current_state = advance(
            current_state,
            adjacent_positions[0],
            diffusion_link_factor[0],
            implicit_solver_matrix[0],
        )
    sea_skin_warmth = current_state[0] * water_indicator
    return_payload = pick_rows(sea_skin_warmth, ocean_slot_row_list.reshape(-1)).reshape(
        blocks, slot_ocean
    )
    back_padding = jnp.zeros_like(return_payload)
    back_outgoing = jnp.concatenate([return_payload, back_padding], axis=0)
    back_incoming = lax.all_to_all(
        back_outgoing, ("comp", "blk"), split_axis=0, concat_axis=0, tiled=True
    )
    back_arrived = back_incoming[blocks:]
    remapped_return = jnp.einsum(
        "okj,oj->ok", backward_weight_blocks[0], back_arrived, precision=lax.Precision.HIGHEST
    )
    atmosphere_surface_temp = add_rows(
        remapped_return.reshape(-1, 1), atm_slot_rows.reshape(-1), cell_count
    )[:, 0]
    flux_out = jnp.where(ocean_section, ocean_flux, atmosphere_flux)
    surface_output = jnp.where(ocean_section, sea_skin_warmth, atmosphere_surface_temp)
    return (current_state[None], flux_out[None], surface_output[None])


def solution(mesh):
    placed = (
        P("comp", None, "blk"),
        P("comp", None, "blk"),
        P("comp", None, "blk"),
        P("comp", None, None),
        P("blk"),
        P(None, "blk"),
        P(),
        P("blk"),
        P("blk", None, None),
        P("blk", None, None),
        P("blk", None, None, None),
        P("blk", None, None, None),
    )
    return jax.shard_map(
        shards,
        mesh=mesh,
        in_specs=placed,
        out_specs=(P("comp", None, "blk"), P("comp", None, "blk"), P("comp", "blk")),
        check_vma=False,
    )
```

profile of v0, /device:TPU:0, one launch (start us, length us, event | category | flops | bytes accessed | tf_op | source)
XLA Modules:
  0.0 710.3 jit_solution(15876248191796628301)
XLA Ops:
  5.6 3.5 copy.70
  9.8 4.2 multiply_bitcast_fusion
  14.0 16.4 %gather_fusion = f32[4096,16]{1,0:T(8,128)} fusion(f32[8192,16]{1,0:T(8,128)} %multiply_bitcast_fusion, s32[4096]{0:T(1024)S(1)} %broadcast_clamp_fusion.1), kind=kCustom, calls=%fused_computation.12 | custom fusion | bytes 540672 | tf_op jit(solution)/shard_map/jit(_take)/gather | solution.py:23
  30.4 3.2 gather.16
  35.0 7.5 %all-to-all-start = ((f32[32,1,4096]{2,1,0:T(1,128)}), f32[32,1,4096]{2,1,0:T(1,128)S(1)}, u32[]{:S(2)}, u32[]{:S(2)}) async-start(f32[32,1,4096]{2,1,0:T(1,128)} %copy.71), calls=%async_computation | async-start | bytes 1048576 | tf_op jit(solution)/shard_map/all_to_all | solution.py:72
  50.3 8.8 %all-to-all-done = f32[32,1,4096]{2,1,0:T(1,128)S(1)} async-done(((f32[32,1,4096]{2,1,0:T(1,128)}), f32[32,1,4096]{2,1,0:T(1,128)S(1)}, u32[]{:S(2)}, u32[]{:S(2)}) %all-to-all-start) | async-done | bytes 524320 | tf_op jit(solution)/shard_map/all_to_all | solution.py:72
  61.8 9.9 %fusion.83 = f32[16,512,16]{1,2,0:T(8,128)S(1)} fusion(f32[16,256,16]{2,1,0:T(8,128)} %reshape.178, f32[1,16,512,256]{3,2,1,0:T(8,128)} %param.26), kind=kOutput, calls=%fused_computation.105 | convolution fusion | flops 402653184 | bytes 9175040 | tf_op jit(solution)/shard_map/ajk,akf->ajf/dot_general | solution.py:75
  71.8 2.7 copy.103
  74.5 46.5 %scatter_custom_fusion = f32[8192,16]{1,0:T(8,128)} fusion(s32[8192]{0:T(1024)S(1)} %bitcast.214, f32[8192,16]{1,0:T(8,128)} %bitcast.183, f32[]{:T(128)} %constant.80.clone.1), kind=kCustom, calls=%fused_computation.77 | custom fusion | flops 131072 | bytes 524800 | tf_op jit(solution)/shard_map/scatter-add | solution.py:28
  121.0 7.2 %fusion.5 = (f32[1,16,8192]{1,2,0:T(8,128)}, f32[8192]{0:T(1024)S(1)}) fusion(f32[8192,16]{1,0:T(8,128)} %scatter_custom_fusion, f32[16,8192]{0,1:T(8,128)} %copy.70, f32[8192]{0:T(1024)S(1)} %copy-done.23, f32[8192]{0:T(1024)S(1)} %copy-done.8, pred[]{:T(512)S(6)} %eq.3, f32[16]{0:T(128)S(1)} %copy-done.43), kind=kLoop, calls=%fused_computation.24 | loop fusion | flops 647168 | bytes 1671233 | tf_op jit(solution)/shard_map/broadcast_in_dim | solution.py:113
  128.5 5.6 collective-permute-start.1
  134.2 8.2 %collective-permute-done = f32[80,1024]{1,0:T(8,128)S(1)} collective-permute-done((f32[80,1024]{1,0:T(8,128)S(1)}, f32[80,1024]{1,0:T(8,128)S(1)}, u32[]{:S(2)}, u32[]{:S(2)}) %collective-permute-start) | collective-permute-done | bytes 327712 | tf_op jit(solution)/shard_map/ppermute | solution.py:16
  146.3 5.6 copy.75
  151.8 30.4 %gather_fusion.7 = f32[8192,80]{1,0:T(8,128)} fusion(f32[80,10240]{0,1:T(8,128)} %copy.75, s32[8192]{0:T(1024)S(1)} %fusion.93), kind=kCustom, calls=%fused_computation.5.clone | custom fusion | bytes 5275648 | tf_op jit(solution)/shard_map/jit(_take)/gather | solution.py:35
  182.2 5.1 copy.86
  187.3 30.4 %gather_fusion.6 = f32[8192,80]{1,0:T(8,128)} fusion(f32[80,10240]{0,1:T(8,128)} %copy.75, s32[8192]{0:T(1024)S(1)} %copy-done.16), kind=kCustom, calls=%fused_computation.4.clone | custom fusion | bytes 5275648 | tf_op jit(solution)/shard_map/jit(_take)/gather | solution.py:35
  217.7 5.1 copy.84
  222.8 30.4 %gather_fusion.5 = f32[8192,80]{1,0:T(8,128)} fusion(f32[80,10240]{0,1:T(8,128)} %copy.75, s32[8192]{0:T(1024)S(1)} %copy-done.12), kind=kCustom, calls=%fused_computation.3.clone | custom fusion | bytes 5275648 | tf_op jit(solution)/shard_map/jit(_take)/gather | solution.py:35
  253.2 5.1 copy.82
  258.3 30.4 %gather_fusion.4 = f32[8192,80]{1,0:T(8,128)} fusion(f32[80,10240]{0,1:T(8,128)} %copy.75, s32[8192]{0:T(1024)S(1)} %copy-done.9), kind=kCustom, calls=%fused_computation.2.clone | custom fusion | bytes 5275648 | tf_op jit(solution)/shard_map/jit(_take)/gather | solution.py:35
  288.7 5.1 copy.80
  293.8 30.4 %gather_fusion.3 = f32[8192,80]{1,0:T(8,128)} fusion(f32[80,10240]{0,1:T(8,128)} %copy.75, s32[8192]{0:T(1024)S(1)} %copy-done.14), kind=kCustom, calls=%fused_computation.1.clone | custom fusion | bytes 5275648 | tf_op jit(solution)/shard_map/jit(_take)/gather | solution.py:35
  324.2 5.1 copy.78
  329.4 30.4 %gather_fusion.2 = f32[8192,80]{1,0:T(8,128)} fusion(f32[80,10240]{0,1:T(8,128)} %copy.75, s32[8192]{0:T(1024)S(1)} %copy-done.10), kind=kCustom, calls=%fused_computation.clone | custom fusion | bytes 5275648 | tf_op jit(solution)/shard_map/jit(_take)/gather | solution.py:35
  359.8 5.2 copy.76
  365.0 8.6 %convolution_bitcast_fusion = f32[80,8192]{1,0:T(8,128)S(1)} fusion(f32[80,8192]{1,0:T(8,128)S(1)} %scatter-add.20, f32[8192,80]{0,1:T(8,128)} %copy.86, f32[8192,80]{0,1:T(8,128)} %copy.84, f32[8192,80]{0,1:T(8,128)} %copy.82, f32[8192,80]{0,1:T(8,128)} %copy.80, f32[8192,80]{0,1:T(8,128)} %copy.78, f32[8192,80]{0,1:T(8,128)} %copy.76, ...), kind=kOutput, calls=%fused_computation.16 | convolution fusion | flops 644874240 | bytes 21242880 | tf_op jit(solution)/shard_map/dot_general | solution.py:38
  375.1 4.3 collective-permute-start.3
  380.0 8.5 %collective-permute-done.2 = f32[80,1024]{1,0:T(8,128)S(1)} collective-permute-done((f32[80,1024]{1,0:T(8,128)S(1)}, f32[80,1024]{1,0:T(8,128)S(1)}, u32[]{:S(2)}, u32[]{:S(2)}) %collective-permute-start.2) | collective-permute-done | bytes 327712 | tf_op jit(solution)/shard_map/ppermute | solution.py:16
  390.6 3.8 copy.87
  394.4 33.1 %gather_fusion.13 = f32[8192,80]{1,0:T(8,128)} fusion(f32[80,10240]{0,1:T(8,128)} %copy.87, s32[8192]{0:T(1024)} %copy-done.18), kind=kCustom, calls=%fused_computation.11.clone | custom fusion | bytes 5275648 | tf_op jit(solution)/shard_map/jit(_take)/gather | solution.py:35
  427.5 30.4 %gather_fusion.12 = f32[8192,80]{1,0:T(8,128)} fusion(f32[80,10240]{0,1:T(8,128)} %copy.87, s32[8192]{0:T(1024)S(1)} %copy-done.17), kind=kCustom, calls=%fused_computation.10.clone | custom fusion | bytes 5275648 | tf_op jit(solution)/shard_map/jit(_take)/gather | solution.py:35
  457.9 30.4 %gather_fusion.11 = f32[8192,80]{1,0:T(8,128)} fusion(f32[80,10240]{0,1:T(8,128)} %copy.87, s32[8192]{0:T(1024)S(1)} %copy-done.13), kind=kCustom, calls=%fused_computation.9.clone | custom fusion | bytes 5275648 | tf_op jit(solution)/shard_map/jit(_take)/gather | solution.py:35
  488.3 30.4 %gather_fusion.10 = f32[8192,80]{1,0:T(8,128)} fusion(f32[80,10240]{0,1:T(8,128)} %copy.87, s32[8192]{0:T(1024)S(1)} %copy-done.9), kind=kCustom, calls=%fused_computation.8.clone | custom fusion | bytes 5275648 | tf_op jit(solution)/shard_map/jit(_take)/gather | solution.py:35
  518.7 30.4 %gather_fusion.9 = f32[8192,80]{1,0:T(8,128)} fusion(f32[80,10240]{0,1:T(8,128)} %copy.87, s32[8192]{0:T(1024)S(1)} %copy-done.15), kind=kCustom, calls=%fused_computation.7.clone | custom fusion | bytes 5275648 | tf_op jit(solution)/shard_map/jit(_take)/gather | solution.py:35
  549.1 30.4 %gather_fusion.8 = f32[8192,80]{1,0:T(8,128)} fusion(f32[80,10240]{0,1:T(8,128)} %copy.87, s32[8192]{0:T(1024)S(1)} %copy-done.11), kind=kCustom, calls=%fused_computation.6.clone | custom fusion | bytes 5275648 | tf_op jit(solution)/shard_map/jit(_take)/gather | solution.py:35
  579.5 5.1 copy.98
  584.6 5.1 copy.96
  589.7 5.1 copy.94
  594.8 5.1 copy.92
  599.9 5.1 copy.90
  605.1 5.3 copy.88
  610.4 8.6 %fusion.9 = f32[8192,80]{0,1:T(8,128)S(1)} fusion(f32[80,8192]{1,0:T(8,128)S(1)} %copy-done.2, f32[8192,80]{0,1:T(8,128)} %copy.98, f32[8192,80]{0,1:T(8,128)} %copy.96, f32[8192,80]{0,1:T(8,128)} %copy.94, f32[8192,80]{0,1:T(8,128)} %copy.92, f32[8192,80]{0,1:T(8,128)} %copy.90, f32[8192,80]{0,1:T(8,128)} %copy.88, f32[8192]{0:T(1024)S(1)} %bitcast.195, ...), kind=kOutput, calls=%fused_computation.32 | convolution fusion | flops 644874240 | bytes 21242880 | tf_op jit(solution)/shard_map/dot_general | solution.py:38
  620.6 45.5 %gather_fusion.1 = f32[8192]{0:T(1024)S(1)} fusion(f32[8192]{0:T(1024)S(1)} %convert_multiply_fusion, s32[8192]{0:T(1024)S(1)} %copy-done.29), kind=kCustom, calls=%fused_computation.13 | custom fusion | bytes 98304 | tf_op jit(solution)/shard_map/jit(_take)/gather | solution.py:23
  666.9 4.2 all-to-all-start.1
  671.0 3.5 copy.99
  674.6 3.8 all-to-all-done.1
  678.4 9.2 %fusion = f32[16,1,256]{2,1,0:T(1,128)S(1)} fusion(f32[1,16,256,512]{3,2,1,0:T(8,128)} %param.27, f32[32,1,512]{2,1,0:T(1,128)S(1)} %all-to-all-done.1), kind=kOutput, calls=%fused_computation.17 | convolution fusion | flops 25165824 | bytes 8437760 | tf_op jit(solution)/shard_map/okj,oj->ok/dot_general | solution.py:105
  687.6 22.1 %scatter_custom_fusion.1 = f32[8192]{0:T(1024)S(1)} fusion(s32[4096]{0:T(1024)} %bitcast.219, f32[4096]{0:T(1024)S(1)} %bitcast.223, f32[]{:T(128)} %constant.80.clone.1), kind=kCustom, calls=%fused_computation.138 | custom fusion | flops 4096 | bytes 33280 | tf_op jit(solution)/shard_map/scatter-add | solution.py:28
  (137 shorter events, 28.7 us)
Async XLA Ops:
  0.6 364.3 %copy-start = (f32[1,80,80]{2,1,0:T(8,128)S(1)}, f32[1,80,80]{2,1,0:T(8,128)}, u32[]{:S(2)}) copy-start(f32[1,80,80]{2,1,0:T(8,128)} %param.19) | copy-start | bytes 76804
  0.6 1.8 copy-start.40
  3.8 5.4 copy-start.42
  30.4 12.1 %copy-start.22 = (s32[1,6,8192]{2,0,1:T(1,128)S(1)}, s32[1,6,8192]{2,0,1:T(1,128)}, u32[]{:S(2)}) copy-start(s32[1,6,8192]{2,0,1:T(1,128)} %param.17) | copy-start | bytes 589828
  33.6 13.3 %copy-start.26 = (s32[1,16,512]{2,1,0:T(8,128)S(1)}, s32[1,16,512]{2,1,0:T(8,128)}, u32[]{:S(2)}) copy-start(s32[1,16,512]{2,1,0:T(8,128)} %param.25) | copy-start | bytes 98308
  33.6 13.3 %copy-start.24 = (s32[8192]{0:T(1024)S(1)}, s32[8192]{0:T(1024)}, u32[]{:S(2)}) copy-start(s32[8192]{0:T(1024)} %param.23) | copy-start | bytes 98308
  35.0 24.1 %all-to-all-start = ((f32[32,1,4096]{2,1,0:T(1,128)}), f32[32,1,4096]{2,1,0:T(1,128)S(1)}, u32[]{:S(2)}, u32[]{:S(2)}) async-start(f32[32,1,4096]{2,1,0:T(1,128)} %copy.71), calls=%async_computation | async-start | bytes 1048576 | tf_op jit(solution)/shard_map/all_to_all | solution.py:72
  43.1 7.2 %copy-start.20 = (s32[1,1,8192]{2,0,1:T(1,128)}, s32[1,1,8192]{2,0,1:T(1,128)S(1)}, u32[]{:S(2)}) copy-start(s32[1,1,8192]{2,0,1:T(1,128)S(1)} %get-tuple-element.42) | copy-start | bytes 98308
  71.8 2.7 copy-start.28
  74.5 46.5 %copy-start.8 = (f32[8192]{0:T(1024)S(1)}, f32[8192]{0:T(1024)}, u32[]{:S(2)}) copy-start(f32[8192]{0:T(1024)} %copy-done.7) | copy-start | bytes 98308
  74.5 46.5 %copy-start.23 = (f32[8192]{0:T(1024)S(1)}, f32[8192]{0:T(1024)}, u32[]{:S(2)}) copy-start(f32[8192]{0:T(1024)} %convert_element_type.3) | copy-start | bytes 98308
  74.5 46.5 %copy-start.43 = (f32[16]{0:T(128)S(1)}, f32[16]{0:T(128)}, u32[]{:S(2)}) copy-start(f32[16]{0:T(128)} %param.22) | copy-start | bytes 196
  120.9 13.2 %copy-start.19 = (s32[1,1,8192]{2,0,1:T(1,128)S(1)}, s32[1,1,8192]{2,0,1:T(1,128)}, u32[]{:S(2)}) copy-start(s32[1,1,8192]{2,0,1:T(1,128)} %get-tuple-element.41) | copy-start | bytes 98308
  121.0 13.2 %copy-start.21 = (s32[1,1,8192]{2,0,1:T(1,128)S(1)}, s32[1,1,8192]{2,0,1:T(1,128)}, u32[]{:S(2)}) copy-start(s32[1,1,8192]{2,0,1:T(1,128)} %copy-done.20) | copy-start | bytes 98308
  128.4 14.0 %collective-permute-start = (f32[80,1024]{1,0:T(8,128)S(1)}, f32[80,1024]{1,0:T(8,128)S(1)}, u32[]{:S(2)}, u32[]{:S(2)}) collective-permute-start(f32[80,1024]{1,0:T(8,128)S(1)} %get-tuple-element.29), channel_id=1, source_target_pairs={{0,1},{1,2},{2,3},{3,4},{4,5},{5,6},{6,7},{7,8},{8,9},{9,10},{10,1... | collective-permute-start | bytes 983048 | tf_op jit(solution)/shard_map/ppermute | solution.py:16
  128.5 15.8 %collective-permute-start.1 = (f32[80,1024]{1,0:T(8,128)S(1)}, f32[80,1024]{1,0:T(8,128)S(1)}, u32[]{:S(2)}, u32[]{:S(2)}) collective-permute-start(f32[80,1024]{1,0:T(8,128)S(1)} %get-tuple-element.30), channel_id=1, source_target_pairs={{1,0},{2,1},{3,2},{4,3},{5,4},{6,5},{7,6},{8,7},{9,8},{10,9},{11,1... | collective-permute-start | bytes 983048 | tf_op jit(solution)/shard_map/ppermute | solution.py:17
  134.1 17.7 %copy-start.18 = (s32[8192]{0:T(1024)}, s32[8192]{0:T(1024)S(1)}, u32[]{:S(2)}) copy-start(s32[8192]{0:T(1024)S(1)} %fusion.93) | copy-start | bytes 98308
  134.2 230.8 %copy-start.36 = (pred[8192]{0:T(1024)(128)(4,1)}, pred[8192]{0:T(1024)(128)(4,1)S(1)}, u32[]{:S(2)}) copy-start(pred[8192]{0:T(1024)(128)(4,1)S(1)} %get-tuple-element.43) | copy-start | bytes 24580
  134.2 230.8 %copy-start.38 = (pred[8192]{0:T(1024)(128)(4,1)}, pred[8192]{0:T(1024)(128)(4,1)S(1)}, u32[]{:S(2)}) copy-start(pred[8192]{0:T(1024)(128)(4,1)S(1)} %get-tuple-element.44) | copy-start | bytes 24580
  182.2 5.1 copy-start.16
  217.7 5.1 copy-start.12
  253.2 5.1 copy-start.9
  288.7 5.1 copy-start.14
  324.2 5.1 copy-start.10
  359.7 5.2 copy-start.4
  359.7 5.2 copy-start.5
  359.7 5.2 copy-start.6
  359.7 5.2 copy-start.30
  359.7 5.2 copy-start.32
  359.8 5.2 copy-start.34
  373.7 16.7 %copy-start.1 = (f32[80,8192]{1,0:T(8,128)}, f32[80,8192]{1,0:T(8,128)S(1)}, u32[]{:S(2)}) copy-start(f32[80,8192]{1,0:T(8,128)S(1)} %convolution_bitcast_fusion) | copy-start | bytes 7864324
  373.7 14.8 %collective-permute-start.2 = (f32[80,1024]{1,0:T(8,128)S(1)}, f32[80,1024]{1,0:T(8,128)S(1)}, u32[]{:S(2)}, u32[]{:S(2)}) collective-permute-start(f32[80,1024]{1,0:T(8,128)S(1)} %get-tuple-element.27), channel_id=1, source_target_pairs={{0,1},{1,2},{2,3},{3,4},{4,5},{5,6},{6,7},{7,8},{8,9},{9,10},{10,1... | collective-permute-start | bytes 983048 | tf_op jit(solution)/shard_map/ppermute | solution.py:16
  375.1 15.3 %collective-permute-start.3 = (f32[80,1024]{1,0:T(8,128)S(1)}, f32[80,1024]{1,0:T(8,128)S(1)}, u32[]{:S(2)}, u32[]{:S(2)}) collective-permute-start(f32[80,1024]{1,0:T(8,128)S(1)} %get-tuple-element.28), channel_id=1, source_target_pairs={{1,0},{2,1},{3,2},{4,3},{5,4},{6,5},{7,6},{8,7},{9,8},{10,9},{11,1... | collective-permute-start | bytes 983048 | tf_op jit(solution)/shard_map/ppermute | solution.py:17
  394.4 33.1 %copy-start.17 = (s32[8192]{0:T(1024)S(1)}, s32[8192]{0:T(1024)}, u32[]{:S(2)}) copy-start(s32[8192]{0:T(1024)} %fusion.92) | copy-start | bytes 98308
  427.5 30.4 %copy-start.13 = (s32[8192]{0:T(1024)S(1)}, s32[8192]{0:T(1024)}, u32[]{:S(2)}) copy-start(s32[8192]{0:T(1024)} %fusion.91) | copy-start | bytes 98308
  488.3 30.4 %copy-start.15 = (s32[8192]{0:T(1024)S(1)}, s32[8192]{0:T(1024)}, u32[]{:S(2)}) copy-start(s32[8192]{0:T(1024)} %fusion.89) | copy-start | bytes 98308
  518.7 30.4 %copy-start.11 = (s32[8192]{0:T(1024)S(1)}, s32[8192]{0:T(1024)}, u32[]{:S(2)}) copy-start(s32[8192]{0:T(1024)} %fusion.88) | copy-start | bytes 98308
  605.1 5.3 copy-start.2
  605.1 5.3 copy-start.31
  605.1 5.3 copy-start.33
  605.1 5.3 copy-start.35
  605.1 5.3 copy-start.37
  605.1 5.3 copy-start.39
  610.4 10.2 %copy-start.25 = (s32[8192]{0:T(1024)S(1)}, s32[8192]{0:T(1024)}, u32[]{:S(2)}) copy-start(s32[8192]{0:T(1024)} %param.23) | copy-start | bytes 98308
  610.4 10.2 %copy-start.29 = (s32[8192]{0:T(1024)S(1)}, s32[8192]{0:T(1024)}, u32[]{:S(2)}) copy-start(s32[8192]{0:T(1024)} %broadcast_clamp_fusion) | copy-start | bytes 98308
  619.1 1.5 copy-start.3
  620.6 45.6 %copy-start.27 = (s32[1,16,512]{2,1,0:T(8,128)S(1)}, s32[1,16,512]{2,1,0:T(8,128)}, u32[]{:S(2)}) copy-start(s32[1,16,512]{2,1,0:T(8,128)} %param.25) | copy-start | bytes 98308
  666.9 11.5 %all-to-all-start.1 = ((f32[32,1,512]{2,1,0:T(1,128)}), f32[32,1,512]{2,1,0:T(1,128)S(1)}, u32[]{:S(2)}, u32[]{:S(2)}) async-start(f32[32,1,512]{2,1,0:T(1,128)} %all_to_all.14), calls=%async_computation.1 | async-start | bytes 131072 | tf_op jit(solution)/shard_map/all_to_all | solution.py:101
  (2 other events, 1.2 us)
where the time goes:
time: 713 us; the launch traced here: 710 us
  local copies, waits for them, and re-layouts  527 us (74%)
  other arithmetic  89.2 us (13%)
  matrix products  36.4 us (5%)
  waiting for transfers between devices  33.1 us (5%)
  starting transfers between devices  23 us (3%)
    gather x24, local copies, waits for them, and re-layouts, advance(): picked = jnp.take(extended, nearby[j], axis=1)  429 us
    scatter-add x2, other arithmetic, add_rows(): return start.at[where].add(values)  68.5 us
    gather x4, local copies, waits for them, and re-layouts, pick_rows(): return jnp.take(table, where, axis=0)  65.1 us
    dot_general x2, matrix products, advance(): return jnp.dot(solver, updated, precision=lax.Precision.HIGHEST)  17.3 us
    ppermute x2, waiting for transfers between devices, with_halo(): before = lax.ppermute(last, axis, up)  16.7 us
  transfers between devices with their start and end apart: 6, of which 6 were waited for; matrix products, arithmetic and copies ran while one was open for 2% of the time, Pallas kernels for 0%

commit v1 on v0

v1 whole, which is shorter than its diff:
```python
import functools

import jax
import jax.numpy as jnp
from jax import lax
from jax.experimental import pallas as pl
from jax.experimental.pallas import tpu as pltpu
from jax.sharding import PartitionSpec as P

HALO = 1024
CHUNK = 128
LANES = 128
SUB = 8
BUFFERS = 4
LIMIT = 56 * 2**20
HIGHEST = lax.Precision.HIGHEST


def to_rows_kernel(field_ref, forcing_ref, rows_ref):
    levels, width = field_ref.shape
    level = lax.broadcasted_iota(jnp.int32, (SUB, LANES), 0)
    for k in range(width // LANES):
        cut = slice(k * LANES, (k + 1) * LANES)
        forcing = jnp.where(level == 0, jnp.broadcast_to(forcing_ref[:, cut], (SUB, LANES)), 0.0)
        block = jnp.concatenate(
            [
                field_ref[:SUB, cut] + forcing,
                field_ref[SUB:, cut],
                jnp.zeros((LANES - levels, LANES), jnp.float32),
            ],
            axis=0,
        )
        rows_ref[cut, :] = block.T


def to_rows(field, forcing, width=1024):
    levels, cells = field.shape
    width = min(width, cells)
    return pl.pallas_call(
        to_rows_kernel,
        grid=(cells // width,),
        in_specs=[
            pl.BlockSpec((levels, width), lambda i: (0, i)),
            pl.BlockSpec((1, width), lambda i: (0, i)),
        ],
        out_specs=pl.BlockSpec((width, LANES), lambda i: (i, 0)),
        out_shape=jax.ShapeDtypeStruct((cells, LANES), jnp.float32),
        compiler_params=pltpu.CompilerParams(vmem_limit_bytes=LIMIT),
        name="to_rows",
    )(field, forcing)


def split(value):
    high = value.astype(jnp.bfloat16)
    return high, (value - high.astype(jnp.float32)).astype(jnp.bfloat16)


def dot_nt(a, b):
    return lax.dot_general(a, b, (((1,), (1,)), ((), ())), preferred_element_type=jnp.float32)


def mix_kernel(pieces, first_chunk, solve, *refs):
    count = len(pieces)
    piece_refs, refs = refs[:count], refs[count:]
    if solve:
        solver_ref, refs = refs[0], refs[1:]
    near_ref, edge_ref, out_ref, table, *slots, near_sems, piece_sems = refs
    neighbours = near_ref.shape[0]
    chunks = out_ref.shape[1 if solve else 0] // CHUNK

    def fetch(i, slot):
        start = pl.multiple_of(first_chunk(i) * CHUNK, CHUNK)
        return pltpu.make_async_copy(
            near_ref.at[:, :, pl.ds(start, CHUNK)], slots[slot], near_sems.at[slot]
        )

    loads = [
        pltpu.make_async_copy(
            ref.at[pl.ds(row, length)], table.at[pl.ds(start, length)], piece_sems.at[k]
        )
        for k, (ref, row, start, length) in enumerate(
            (piece_refs[k], row, start, length) for k, (row, start, length) in enumerate(pieces)
        )
    ]
    for load in loads:
        load.start()
    for slot in range(BUFFERS - 1):
        fetch(slot, slot).start()
    for load in loads:
        load.wait()
    lane_sub = lax.broadcasted_iota(jnp.int32, (SUB, LANES), 0)
    masks = [lane_sub == s for s in range(SUB)]

    def body(turn, carry):
        for slot in range(BUFFERS):
            i = turn * BUFFERS + slot
            fetch(i, slot).wait()

            @pl.when(i + BUFFERS - 1 < chunks)
            def _():
                fetch(i + BUFFERS - 1, (slot + BUFFERS - 1) % BUFFERS).start()

            cell = pl.multiple_of(first_chunk(i) * CHUNK, CHUNK)
            edges = [edge_ref[j, :, pl.ds(cell, CHUNK)] for j in range(neighbours)]
            keep = 1.0 - functools.reduce(lambda a, b: a + b, edges)
            stacked = jnp.concatenate(
                edges + [keep, jnp.zeros((SUB - neighbours - 1, CHUNK), jnp.float32)], axis=0
            )
            factors = stacked.T
            mixed = []
            for g in range(CHUNK // SUB):
                own = table[pl.ds(pl.multiple_of(HALO + cell + g * SUB, SUB), SUB), :]
                part = factors[g * SUB : (g + 1) * SUB]
                total = jnp.broadcast_to(part[:, neighbours : neighbours + 1], (SUB, LANES)) * own
                for j in range(neighbours):
                    picked = None
                    for s in range(SUB):
                        where = slots[slot][j, 0, g * SUB + s]
                        row = jnp.broadcast_to(table[pl.ds(where, 1), :], (SUB, LANES))
                        picked = row if s == 0 else jnp.where(masks[s], row, picked)
                    total = total + jnp.broadcast_to(part[:, j : j + 1], (SUB, LANES)) * picked
                if solve:
                    mixed.append(total)
                else:
                    out_ref[pl.ds(pl.multiple_of(i * CHUNK + g * SUB, SUB), SUB), :] = total
            if solve:
                high, low = split(jnp.concatenate(mixed, axis=0))
                solver_high, solver_low = split(solver_ref[...])
                out_ref[:, pl.ds(pl.multiple_of(i * CHUNK, CHUNK), CHUNK)] = (
                    dot_nt(solver_high, low) + dot_nt(solver_low, high)
                ) + dot_nt(solver_high, high)
        return carry

    lax.fori_loop(0, chunks // BUFFERS, body, 0)


def mix(pieces, near, edges, chunk_of, chunks, solver=None):
    rows = sum(length for _, _, _, length in pieces)
    anywhere = pl.BlockSpec(memory_space=pl.ANY)
    solve = solver is not None
    if solve:
        out_shape = jax.ShapeDtypeStruct((solver.shape[0], chunks * CHUNK), jnp.float32)
    else:
        out_shape = jax.ShapeDtypeStruct((chunks * CHUNK, LANES), jnp.float32)
    return pl.pallas_call(
        functools.partial(
            mix_kernel,
            [(row, start, length) for _, row, start, length in pieces],
            chunk_of,
            solve,
        ),
        in_specs=[anywhere] * len(pieces)
        + [pl.BlockSpec(memory_space=pltpu.VMEM)] * (1 if solve else 0)
        + [anywhere, pl.BlockSpec(memory_space=pltpu.VMEM)],
        out_specs=pl.BlockSpec(memory_space=pltpu.VMEM),
        out_shape=out_shape,
        scratch_shapes=[pltpu.VMEM((rows, LANES), jnp.float32)]
        + [pltpu.SMEM((near.shape[0], 1, CHUNK), jnp.int32)] * BUFFERS
        + [pltpu.SemaphoreType.DMA((BUFFERS,)), pltpu.SemaphoreType.DMA((len(pieces),))],
        compiler_params=pltpu.CompilerParams(vmem_limit_bytes=LIMIT),
        name="mix_solve" if solve else "mix",
    )(*[array for array, _, _, _ in pieces], *([solver] if solve else []), near, edges)


def to_neighbours(initial, last):
    count = lax.axis_size("blk")
    up = [(i, (i + 1) % count) for i in range(count)]
    down = [(j, i) for i, j in up]
    return lax.ppermute(last, "blk", up), lax.ppermute(initial, "blk", down)


def pick_rows(table, where):
    return jnp.take(table, where, axis=0)


def add_rows(values, where, count):
    start = jnp.zeros((count, values.shape[1]), jnp.float32)
    return start.at[where].add(values)


def shards(
    thermal_profiles,
    adjacent_positions,
    diffusion_link_factor,
    implicit_solver_matrix,
    lagged_surface_temp,
    flux_coefficient,
    flux_heating,
    ocean_cell_mask,
    atmosphere_slot_cells,
    ocean_slot_cells,
    forward_weight_blocks,
    backward_weight_blocks,
):
    blocks = lax.axis_size("blk")
    ocean_section = lax.axis_index("comp") == 1
    water_indicator = ocean_cell_mask.astype(jnp.float32)
    owner_state = thermal_profiles[0]
    level_stack, cell_count = owner_state.shape
    flux_count = flux_coefficient.shape[0]
    neighbours = adjacent_positions.shape[1]
    near = adjacent_positions.reshape(neighbours, 1, cell_count)
    edges = diffusion_link_factor.reshape(neighbours, 1, cell_count)
    solver = implicit_solver_matrix[0]

    before, after = to_neighbours(owner_state[:, :HALO], owner_state[:, cell_count - HALO :])

    atmosphere_flux = (
        flux_coefficient * (owner_state[level_stack - 1] - lagged_surface_temp)[None, :]
    )
    atm_slot_rows = atmosphere_slot_cells[0]
    slot_atm = atm_slot_rows.shape[1]
    payload = pick_rows(atmosphere_flux.T, atm_slot_rows.reshape(-1)).reshape(
        blocks, slot_atm * flux_count
    )
    padding = jnp.zeros_like(payload)
    outgoing = jnp.concatenate([padding, payload], axis=0)
    incoming = lax.all_to_all(outgoing, ("comp", "blk"), split_axis=0, concat_axis=0, tiled=True)
    arrived = incoming[:blocks]
    arrived_rows = arrived.reshape(blocks, slot_atm, flux_count)
    mapped = jnp.einsum("ajk,akf->ajf", forward_weight_blocks[0], arrived_rows, precision=HIGHEST)
    ocean_slot_row_list = ocean_slot_cells[0]
    slot_ocean = ocean_slot_row_list.shape[1]
    ocean_rows = add_rows(
        mapped.reshape(blocks * slot_ocean, flux_count), ocean_slot_row_list.reshape(-1), cell_count
    )
    ocean_flux = ocean_rows.T * water_indicator[None, :]
    driving_source = jnp.sum(flux_heating[:, None] * ocean_flux, axis=0)
    forcing = jnp.where(ocean_section, driving_source, jnp.zeros_like(driving_source))[None, :]

    forcing_before, forcing_after = to_neighbours(
        forcing[:, :HALO], forcing[:, cell_count - HALO :]
    )
    rows = to_rows(owner_state, forcing)
    rows_before = to_rows(before, forcing_before)
    rows_after = to_rows(after, forcing_after)

    halo_chunks = HALO // CHUNK
    chunks = cell_count // CHUNK
    middle = cell_count - 2 * HALO
    first_table = [
        (rows_before, 0, 0, HALO),
        (rows, 0, HALO, cell_count),
        (rows_after, 0, HALO + cell_count, HALO),
    ]
    rims = mix(
        first_table,
        near,
        edges,
        lambda i: jnp.where(i < halo_chunks, i, i + chunks - 2 * halo_chunks),
        2 * halo_chunks,
    )
    next_before, next_after = to_neighbours(rims[:HALO], rims[HALO:])
    inside = mix(first_table, near, edges, lambda i: i + halo_chunks, chunks - 2 * halo_chunks)
    second_table = [
        (next_before, 0, 0, HALO),
        (rims, 0, HALO, HALO),
        (inside, 0, 2 * HALO, middle),
        (rims, HALO, 2 * HALO + middle, HALO),
        (next_after, 0, HALO + cell_count, HALO),
    ]
    twice = jnp.dot(solver, solver, precision=HIGHEST)
    twice = jnp.pad(twice, ((0, 0), (0, LANES - level_stack)))
    current_state = mix(second_table, near, edges, lambda i: i, chunks, twice)

    sea_skin_warmth = current_state[0] * water_indicator
    return_payload = pick_rows(sea_skin_warmth, ocean_slot_row_list.reshape(-1)).reshape(
        blocks, slot_ocean
    )
    back_padding = jnp.zeros_like(return_payload)
    back_outgoing = jnp.concatenate([return_payload, back_padding], axis=0)
    back_incoming = lax.all_to_all(
        back_outgoing, ("comp", "blk"), split_axis=0, concat_axis=0, tiled=True
    )
    back_arrived = back_incoming[blocks:]
    remapped_return = jnp.einsum(
        "okj,oj->ok", backward_weight_blocks[0], back_arrived, precision=HIGHEST
    )
    atmosphere_surface_temp = add_rows(
        remapped_return.reshape(-1, 1), atm_slot_rows.reshape(-1), cell_count
    )[:, 0]
    flux_out = jnp.where(ocean_section, ocean_flux, atmosphere_flux)
    surface_output = jnp.where(ocean_section, sea_skin_warmth, atmosphere_surface_temp)
    return (current_state[None], flux_out[None], surface_output[None])


def solution(mesh):
    placed = (
        P("comp", None, "blk"),
        P("comp", None, "blk"),
        P("comp", None, "blk"),
        P("comp", None, None),
        P("blk"),
        P(None, "blk"),
        P(),
        P("blk"),
        P("blk", None, None),
        P("blk", None, None),
        P("blk", None, None, None),
        P("blk", None, None, None),
    )
    return jax.shard_map(
        shards,
        mesh=mesh,
        in_specs=placed,
        out_specs=(P("comp", None, "blk"), P("comp", None, "blk"), P("comp", "blk")),
        check_vma=False,
    )
```

time: 713 us -> 341 us (0.48)
  local copies, waits for them, and re-layouts: 527 us -> 84.2 us
  Pallas kernels: 0 us -> 110 us
  matrix products: 36.4 us -> 19 us
  waiting for transfers between devices: 33.1 us -> 20.3 us
  other arithmetic: 89.2 us -> 81.3 us
    gather x24 -> x0, local copies, waits for them, and re-layouts: 429 us -> none  [advance(): picked = jnp.take(extended, nearby[j], axis=1)]
    pallas_call x0 -> x6, Pallas kernels: none -> 110 us  [the longest x3 98.8 us: mix(): pl.pallas_call(functools.partial(mix_kernel, [(row, start, length) for _,...]
    ppermute x4 -> x6, waiting for transfers between devices: 20.5 us -> 0.02 us  [to_neighbours(): return (lax.ppermute(last, 'blk', up), lax.ppermute(initial, 'blk', down))]
    dot_general x2 -> x1, matrix products: 17.3 us -> 0.17 us  [shards(): twice = jnp.dot(solver, solver, precision=HIGHEST)]
    concatenate x2 -> x0, local copies, waits for them, and re-layouts: 9.36 us -> none  [with_halo(): shard = jnp.concatenate([before, shard, after], axis=dim)]
    all_to_all x1, waiting for transfers between devices: 8.84 us -> 16.5 us  [shards(): lax.all_to_all(outgoing, ('comp', 'blk'), split_axis=0, concat_axis=0, ti...]
    ppermute x4 -> x6, starting transfers between devices: 11.3 us -> 14.7 us  [to_neighbours(): return (lax.ppermute(last, 'blk', up), lax.ppermute(initial, 'blk', down))]
  transfers between devices with their start and end apart: 6 -> 8, of which waited for: 6 -> 2; matrix products, arithmetic and copies ran while one was open for 2% -> 29% of each run, Pallas kernels for 0% -> 12%
where the time goes in v1:
time: 341 us; the launch traced here: 340 us
  Pallas kernels  110 us (32%)
  local copies, waits for them, and re-layouts  84.2 us (25%)
  other arithmetic  81.3 us (24%)
  starting transfers between devices  25.1 us (7%)
  waiting for transfers between devices  20.3 us (6%)
  matrix products  19 us (6%)
    pallas_call x3, Pallas kernels, mix(): pl.pallas_call(functools.partial(mix_kernel, [(row, start, length) for _,...  98.8 us
    scatter-add x2, other arithmetic, add_rows(): return start.at[where].add(values)  68.4 us
    gather x4, local copies, waits for them, and re-layouts, pick_rows(): return jnp.take(table, where, axis=0)  60.1 us
    all_to_all x1, waiting for transfers between devices, shards(): lax.all_to_all(outgoing, ('comp', 'blk'), split_axis=0, concat_axis=0, ti...  16.5 us
    ppermute x6, starting transfers between devices, to_neighbours(): return (lax.ppermute(last, 'blk', up), lax.ppermute(initial, 'blk', down))  14.7 us
    pallas_call x3, Pallas kernels, to_rows(): pl.pallas_call(to_rows_kernel, grid=(cells // width,), in_specs=[pl.Block...  10.7 us
    unnamed x25, local copies, waits for them, and re-layouts  10.6 us
    dot_general x1, matrix products, shards(): jnp.einsum('ajk,akf->ajf', forward_weight_blocks[0], arrived_rows, precis...  9.61 us
  transfers between devices with their start and end apart: 8, of which 2 were waited for; matrix products, arithmetic and copies ran while one was open for 29% of the time, Pallas kernels for 12%

profile of v1, /device:TPU:0, one launch (start us, length us, event | category | flops | bytes accessed | tf_op | source)
XLA Modules:
  0.0 340.4 jit_solution(8869505121263580411)
XLA Ops:
  0.6 0.0 copy-start
  0.7 1.1 fusion.15
  1.8 7.0 %collective-permute-start.2 = (f32[80,1024]{1,0:T(8,128)S(1)}, f32[80,1024]{1,0:T(8,128)}, u32[]{:S(2)}, u32[]{:S(2)}) collective-permute-start(f32[80,1024]{1,0:T(8,128)S(1)} %get-tuple-element.14), channel_id=1, source_target_pairs={{1,0},{2,1},{3,2},{4,3},{5,4},{6,5},{7,6},{8,7},{9,8},{10,9},{11,1... | collective-permute-start | bytes 983048 | tf_op jit(solution)/shard_map/ppermute | solution.py:169
  8.8 1.0 slice.36
  9.8 0.7 compare_and_fusion
  10.5 0.7 copy.34
  11.3 0.7 broadcast_in_dim.45
  12.0 1.8 broadcast_in_dim.46
  13.8 3.5 %copy.22 = f32[16,8192]{0,1:T(8,128)} copy(f32[16,8192]{1,0:T(8,128)} %param.17) | data formatting | bytes 1048576 | tf_op args[5]
  17.3 4.2 %multiply_bitcast_fusion = f32[8192,16]{1,0:T(8,128)} fusion(f32[16,8192]{0,1:T(8,128)} %copy.22, f32[8192]{0:T(1024)S(1)} %sub.3), kind=kLoop, calls=%fused_computation.12 | loop fusion | flops 131072 | bytes 1081344 | tf_op jit(solution)/shard_map/transpose | solution.py:213
  21.5 13.0 %gather_fusion = f32[4096,16]{1,0:T(8,128)S(1)} fusion(f32[8192,16]{1,0:T(8,128)} %multiply_bitcast_fusion, s32[4096]{0:T(1024)S(1)} %broadcast_clamp_fusion.1), kind=kCustom, calls=%fused_computation | custom fusion | bytes 540672 | tf_op jit(solution)/shard_map/jit(_take)/gather | solution.py:173
  34.5 0.0 copy-start.4
  34.5 1.6 gather.13
  36.1 1.3 copy.23
  37.5 6.2 %all-to-all-start = ((f32[32,1,4096]{2,1,0:T(1,128)}), f32[32,1,4096]{2,1,0:T(1,128)S(1)}, u32[]{:S(2)}, u32[]{:S(2)}) async-start(f32[32,1,4096]{2,1,0:T(1,128)} %copy.23), calls=%async_computation | async-start | bytes 1048576 | tf_op jit(solution)/shard_map/all_to_all | solution.py:218
  43.8 16.5 %all-to-all-done = f32[32,1,4096]{2,1,0:T(1,128)S(1)} async-done(((f32[32,1,4096]{2,1,0:T(1,128)}), f32[32,1,4096]{2,1,0:T(1,128)S(1)}, u32[]{:S(2)}, u32[]{:S(2)}) %all-to-all-start) | async-done | bytes 524320 | tf_op jit(solution)/shard_map/all_to_all | solution.py:218
  60.3 0.7 slice_reduce_fusion
  60.9 0.7 reshape.119
  61.7 9.6 %fusion.8 = f32[16,512,16]{1,2,0:T(8,128)S(1)} fusion(f32[16,256,16]{2,1,0:T(8,128)S(1)} %reshape.119, f32[1,16,512,256]{3,2,1,0:T(8,128)} %param.22), kind=kOutput, calls=%fused_computation.15 | convolution fusion | flops 402653184 | bytes 9175040 | tf_op jit(solution)/shard_map/ajk,akf->ajf/dot_general | solution.py:221
  71.3 2.6 copy.31
  73.9 46.5 %scatter_custom_fusion = f32[8192,16]{1,0:T(8,128)} fusion(s32[8192]{0:T(1024)S(1)} %bitcast.75, f32[8192,16]{1,0:T(8,128)} %bitcast.60, f32[]{:T(128)} %constant.18.clone.1), kind=kCustom, calls=%fused_computation.13 | custom fusion | flops 131072 | bytes 524800 | tf_op jit(solution)/shard_map/scatter-add | solution.py:178
  120.4 7.2 %fusion.5 = (f32[1,16,8192]{1,2,0:T(8,128)}, f32[8192]{0:T(1024)S(1)}) fusion(f32[8192,16]{1,0:T(8,128)} %scatter_custom_fusion, f32[16,8192]{0,1:T(8,128)} %copy.22, f32[8192]{0:T(1024)S(1)} %convert_element_type.5, f32[8192]{0:T(1024)S(1)} %sub.3, pred[]{:T(512)S(6)} %eq.3, f32[16]{0:T(128)S(1)} %copy-done.9), kind=kLoop, calls=%fused_computation.11 | loop fusion | flops 647168 | bytes 1671233 | tf_op jit(solution)/shard_map/broadcast_in_dim | solution.py:284
  127.6 0.1 collective-permute-start.1
  127.7 5.6 %collective-permute-start.3 = (f32[1,1024]{1,0:T(1,128)S(1)}, f32[1,1024]{1,0:T(1,128)S(1)}, u32[]{:S(2)}, u32[]{:S(2)}) collective-permute-start(f32[1,1024]{1,0:T(1,128)S(1)} %get-tuple-element.18), channel_id=1, source_target_pairs={{1,0},{2,1},{3,2},{4,3},{5,4},{6,5},{7,6},{8,7},{9,8},{10,9},{11,1... | collective-permute-start | bytes 12296 | tf_op jit(solution)/shard_map/ppermute | solution.py:169
  133.3 6.8 %to_rows.4.refs_1_ = f32[8192,128]{1,0:T(8,128)} custom-call(f32[80,8192]{1,0:T(8,128)} %bitcast.62, f32[1,8192]{1,0:T(1,128)} %bitcast.71), custom_call_target="tpu_custom_call" | custom-call | tf_op jit(solution)/shard_map/to_rows/pallas_call | solution.py:39
  140.1 0.6 copy-done.8
  140.7 2.0 to_rows.3.refs_0_
  142.7 0.6 copy-done.7
  143.3 2.0 to_rows.5.refs_2_
  145.3 13.3 %mix.2.refs_1_.refs_3_ = f32[2048,128]{1,0:T(8,128)} custom-call(f32[1024,128]{1,0:T(8,128)} %to_rows.3.refs_0_, f32[8192,128]{1,0:T(8,128)} %to_rows.4.refs_1_, f32[1024,128]{1,0:T(8,128)} %to_rows.5.refs_2_, s32[6,1,8192]{2,1,0:T(1,128)} %bitcast.64, f32[6,1,8192]{2,1,0:T(1,128)} %bitcast.67), custom_call_target="tpu_custom_call" | custom-call | tf_op jit(solution)/shard_map/mix/pallas_call | solution.py:145
  158.6 1.3 fusion.16
  159.9 0.1 collective-permute-start.5
  159.9 2.0 collective-permute-start.4
  161.9 0.2 fusion.11
  162.1 0.6 pad.6.refs_5_
  162.7 31.7 %mix.3.refs_2_ = f32[6144,128]{1,0:T(8,128)} custom-call(f32[1024,128]{1,0:T(8,128)} %to_rows.3.refs_0_, f32[8192,128]{1,0:T(8,128)} %to_rows.4.refs_1_, f32[1024,128]{1,0:T(8,128)} %to_rows.5.refs_2_, s32[6,1,8192]{2,1,0:T(1,128)} %bitcast.65, f32[6,1,8192]{2,1,0:T(1,128)} %bitcast.68), custom_call_target="tpu_custom_call" | custom-call | tf_op jit(solution)/shard_map/mix/pallas_call | solution.py:145
  194.5 0.8 copy-done.1
  195.3 0.8 copy-done.2
  196.0 53.8 %mix_solve.1 = f32[80,8192]{1,0:T(8,128)} custom-call(f32[1024,128]{1,0:T(8,128)} %copy-done.2, f32[2048,128]{1,0:T(8,128)} %mix.2.refs_1_.refs_3_, f32[6144,128]{1,0:T(8,128)} %mix.3.refs_2_, f32[2048,128]{1,0:T(8,128)} %mix.2.refs_1_.refs_3_, f32[1024,128]{1,0:T(8,128)} %copy-done.1, f32[80,128]{1,0:T(8,128)} %pad.6.refs_5_, s32[6,1,8192]{2,1,0:T(1,128)} %bitcast.66, ...), custom_call_target="tpu_custom_call" | custom-call | tf_op jit(solution)/shard_map/mix_solve/pallas_call | solution.py:145
  249.8 1.0 slice.57
  250.8 45.5 %gather_fusion.1 = f32[8192]{0:T(1024)S(1)} fusion(f32[8192]{0:T(1024)S(1)} %convert_multiply_fusion, s32[8192]{0:T(1024)S(1)} %broadcast_clamp_fusion), kind=kCustom, calls=%fused_computation.1 | custom fusion | bytes 98304 | tf_op jit(solution)/shard_map/jit(_take)/gather | solution.py:173
  296.4 0.7 all_to_all.14
  297.1 4.2 %all-to-all-start.1 = ((f32[32,1,512]{2,1,0:T(1,128)}), f32[32,1,512]{2,1,0:T(1,128)S(1)}, u32[]{:S(2)}, u32[]{:S(2)}) async-start(f32[32,1,512]{2,1,0:T(1,128)} %all_to_all.14), calls=%async_computation.1 | async-start | bytes 131072 | tf_op jit(solution)/shard_map/all_to_all | solution.py:272
  301.3 3.5 %copy.27 = f32[1,16,8192]{2,1,0:T(8,128)} copy(f32[1,16,8192]{1,2,0:T(8,128)} %get-tuple-element.12) | data formatting | bytes 1048576
  304.8 3.8 %all-to-all-done.1 = f32[32,1,512]{2,1,0:T(1,128)S(1)} async-done(((f32[32,1,512]{2,1,0:T(1,128)}), f32[32,1,512]{2,1,0:T(1,128)S(1)}, u32[]{:S(2)}, u32[]{:S(2)}) %all-to-all-start.1) | async-done | bytes 65568 | tf_op jit(solution)/shard_map/all_to_all | solution.py:272
  308.6 9.2 %fusion = f32[16,1,256]{2,1,0:T(1,128)S(1)} fusion(f32[1,16,256,512]{3,2,1,0:T(8,128)} %param.23, f32[32,1,512]{2,1,0:T(1,128)S(1)} %all-to-all-done.1), kind=kOutput, calls=%fused_computation.4 | convolution fusion | flops 25165824 | bytes 8437760 | tf_op jit(solution)/shard_map/okj,oj->ok/dot_general | solution.py:276
  317.9 21.9 %scatter_custom_fusion.1 = f32[8192]{0:T(1024)S(1)} fusion(s32[4096]{0:T(1024)S(1)} %bitcast.80, f32[4096]{0:T(1024)S(1)} %bitcast.84, f32[]{:T(128)} %constant.18.clone.1), kind=kCustom, calls=%fused_computation.29 | custom fusion | flops 4096 | bytes 32772 | tf_op jit(solution)/shard_map/scatter-add | solution.py:178
  339.8 0.6 broadcast_select_fusion.2
  (38 shorter events, 0.3 us)
Async XLA Ops:
  0.6 161.3 %copy-start = (f32[1,80,80]{2,1,0:T(8,128)S(1)}, f32[1,80,80]{2,1,0:T(8,128)}, u32[]{:S(2)}) copy-start(f32[1,80,80]{2,1,0:T(8,128)} %param.15) | copy-start | bytes 76804
  0.6 16.6 %copy-start.6 = (f32[8192]{0:T(1024)S(1)}, f32[8192]{0:T(1024)}, u32[]{:S(2)}) copy-start(f32[8192]{0:T(1024)} %param.16) | copy-start | bytes 98308
  1.8 140.9 %collective-permute-start.2 = (f32[80,1024]{1,0:T(8,128)S(1)}, f32[80,1024]{1,0:T(8,128)}, u32[]{:S(2)}, u32[]{:S(2)}) collective-permute-start(f32[80,1024]{1,0:T(8,128)S(1)} %get-tuple-element.14), channel_id=1, source_target_pairs={{1,0},{2,1},{3,2},{4,3},{5,4},{6,5},{7,6},{8,7},{9,8},{10,9},{11,1... | collective-permute-start | bytes 983048 | tf_op jit(solution)/shard_map/ppermute | solution.py:169
  8.8 131.3 %collective-permute-start = (f32[80,1024]{1,0:T(8,128)S(1)}, f32[80,1024]{1,0:T(8,128)}, u32[]{:S(2)}, u32[]{:S(2)}) collective-permute-start(f32[80,1024]{1,0:T(8,128)S(1)} %get-tuple-element.15), channel_id=1, source_target_pairs={{0,1},{1,2},{2,3},{3,4},{4,5},{5,6},{6,7},{7,8},{8,9},{9,10},{10,1... | collective-permute-start | bytes 983048 | tf_op jit(solution)/shard_map/ppermute | solution.py:169
  34.5 9.2 %copy-start.5 = (s32[1,16,512]{2,1,0:T(8,128)S(1)}, s32[1,16,512]{2,1,0:T(8,128)}, u32[]{:S(2)}) copy-start(s32[1,16,512]{2,1,0:T(8,128)} %param.21) | copy-start | bytes 98308
  34.5 9.2 %copy-start.4 = (s32[8192]{0:T(1024)S(1)}, s32[8192]{0:T(1024)}, u32[]{:S(2)}) copy-start(s32[8192]{0:T(1024)} %param.19) | copy-start | bytes 98308
  37.5 22.8 %all-to-all-start = ((f32[32,1,4096]{2,1,0:T(1,128)}), f32[32,1,4096]{2,1,0:T(1,128)S(1)}, u32[]{:S(2)}, u32[]{:S(2)}) async-start(f32[32,1,4096]{2,1,0:T(1,128)} %copy.23), calls=%async_computation | async-start | bytes 1048576 | tf_op jit(solution)/shard_map/all_to_all | solution.py:218
  71.3 49.1 %copy-start.9 = (f32[16]{0:T(128)S(1)}, f32[16]{0:T(128)}, u32[]{:S(2)}) copy-start(f32[16]{0:T(128)} %param.18) | copy-start | bytes 196
  127.6 5.7 %copy-start.3 = (f32[8192]{0:T(1024)}, f32[8192]{0:T(1024)S(1)}, u32[]{:S(2)}) copy-start(f32[8192]{0:T(1024)S(1)} %broadcast_select_fusion.1) | copy-start | bytes 98308
  127.6 12.5 %collective-permute-start.1 = (f32[1,1024]{1,0:T(1,128)S(1)}, f32[1,1024]{1,0:T(1,128)S(1)}, u32[]{:S(2)}, u32[]{:S(2)}) collective-permute-start(f32[1,1024]{1,0:T(1,128)S(1)} %get-tuple-element.19), channel_id=1, source_target_pairs={{0,1},{1,2},{2,3},{3,4},{4,5},{5,6},{6,7},{7,8},{8,9},{9,10},{10,1... | collective-permute-start | bytes 12296 | tf_op jit(solution)/shard_map/ppermute | solution.py:169
  127.7 15.0 %collective-permute-start.3 = (f32[1,1024]{1,0:T(1,128)S(1)}, f32[1,1024]{1,0:T(1,128)S(1)}, u32[]{:S(2)}, u32[]{:S(2)}) collective-permute-start(f32[1,1024]{1,0:T(1,128)S(1)} %get-tuple-element.18), channel_id=1, source_target_pairs={{1,0},{2,1},{3,2},{4,3},{5,4},{6,5},{7,6},{8,7},{9,8},{10,9},{11,1... | collective-permute-start | bytes 12296 | tf_op jit(solution)/shard_map/ppermute | solution.py:169
  140.1 0.6 copy-start.8
  142.7 0.6 copy-start.7
  159.9 34.6 %collective-permute-start.5 = (f32[1024,128]{1,0:T(8,128)S(1)}, f32[1024,128]{1,0:T(8,128)S(1)}, u32[]{:S(2)}, u32[]{:S(2)}) collective-permute-start(f32[1024,128]{1,0:T(8,128)S(1)} %get-tuple-element.16), channel_id=1, source_target_pairs={{1,0},{2,1},{3,2},{4,3},{5,4},{6,5},{7,6},{8,7},{9,8},{10,9},{11,1... | collective-permute-start | bytes 1572872 | tf_op jit(solution)/shard_map/ppermute | solution.py:169
  159.9 34.5 %collective-permute-start.4 = (f32[1024,128]{1,0:T(8,128)S(1)}, f32[1024,128]{1,0:T(8,128)S(1)}, u32[]{:S(2)}, u32[]{:S(2)}) collective-permute-start(f32[1024,128]{1,0:T(8,128)S(1)} %get-tuple-element.17), channel_id=1, source_target_pairs={{0,1},{1,2},{2,3},{3,4},{4,5},{5,6},{6,7},{7,8},{8,9},{9,10},{10,1... | collective-permute-start | bytes 1572872 | tf_op jit(solution)/shard_map/ppermute | solution.py:169
  194.4 0.8 copy-start.1
  195.3 0.8 copy-start.2
  297.1 11.6 %all-to-all-start.1 = ((f32[32,1,512]{2,1,0:T(1,128)}), f32[32,1,512]{2,1,0:T(1,128)S(1)}, u32[]{:S(2)}, u32[]{:S(2)}) async-start(f32[32,1,512]{2,1,0:T(1,128)} %all_to_all.14), calls=%async_computation.1 | async-start | bytes 131072 | tf_op jit(solution)/shard_map/all_to_all | solution.py:272

commit v2 on v0

v2 whole, which is shorter than its diff:
```python
import functools

import jax
import jax.numpy as jnp
from jax import lax
from jax.experimental import pallas as pl
from jax.experimental.pallas import tpu as pltpu
from jax.sharding import PartitionSpec as P

HALO = 1024
CHUNK = 128
LANES = 128
WIDE = 256
SUB = 8
BUFFERS = 4
GROUP = 4
LIMIT = 56 * 2**20
HIGHEST = lax.Precision.HIGHEST


def split(value):
    high = value.astype(jnp.bfloat16)
    return high, (value - high.astype(jnp.float32)).astype(jnp.bfloat16)


def dot(a, b):
    return jnp.dot(a, b, preferred_element_type=jnp.float32)


def dot_nt(a, b):
    return lax.dot_general(a, b, (((1,), (1,)), ((), ())), preferred_element_type=jnp.float32)


def params():
    return pltpu.CompilerParams(vmem_limit_bytes=LIMIT)


def whole():
    return pl.BlockSpec(memory_space=pltpu.VMEM)


def scalars():
    return pl.BlockSpec(memory_space=pltpu.SMEM)


def anywhere():
    return pl.BlockSpec(memory_space=pl.ANY)


def lanes_from(row, lane):
    return jnp.take_along_axis(row, lane, axis=1)


def pick_lanes(count, tables, cells, parts=4):
    high, low = cells >> 7, cells & (LANES - 1)
    totals = []
    for part in range(parts):
        found = [jnp.zeros(cells.shape, jnp.float32) for _ in tables]
        for tile in range(part, count, parts):
            here = high == tile
            found = [
                jnp.where(here, lanes_from(table(tile), low), seen)
                for table, seen in zip(tables, found)
            ]
        totals.append(found)
    return [functools.reduce(lambda a, b: a + b, column) for column in zip(*totals)]


def pack_kernel(
    ocean_ref, coefficient_ref, own_ref, received_ref, lagged_ref, slot_ref, flux_ref, payload_ref
):
    fields, cells = coefficient_ref.shape
    for k in range(cells // LANES):
        cut = slice(k * LANES, (k + 1) * LANES)
        air = jnp.where(ocean_ref[0] == 1, received_ref[:, cut], own_ref[:, cut])
        flux_ref[:, cut] = coefficient_ref[:, cut] * (air - lagged_ref[:, cut])
    owners, slots = slot_ref.shape
    width = min(slots, LANES)
    pieces = slots // width

    def tile_of(base, k):
        return flux_ref[base : base + SUB, k * LANES : (k + 1) * LANES]

    tables = [functools.partial(tile_of, base) for base in range(0, fields, SUB)]

    def body(owner, carry):
        row = slot_ref[pl.ds(owner, 1), :]
        for piece in range(pieces):
            where = row[:, piece * width : (piece + 1) * width]
            if width < LANES:
                where = jnp.concatenate([where] * (LANES // width), axis=1)
            where = jnp.broadcast_to(where, (SUB, LANES))
            for n, found in enumerate(pick_lanes(cells // LANES, tables, where)):
                payload_ref[owner, n * SUB : (n + 1) * SUB, piece * width : (piece + 1) * width] = (
                    found[:, :width]
                )
        return carry

    lax.fori_loop(0, owners, body, 0, unroll=2)


def pack(ocean, coefficient, own, received, lagged, slots):
    fields, cells = coefficient.shape
    owners, count = slots.shape
    return pl.pallas_call(
        pack_kernel,
        in_specs=[scalars()] + [whole()] * 5,
        out_specs=[whole()] * 2,
        out_shape=[
            jax.ShapeDtypeStruct((fields, cells), jnp.float32),
            jax.ShapeDtypeStruct((owners, fields, count), jnp.float32),
        ],
        compiler_params=params(),
        name="pack",
    )(ocean, coefficient, own, received, lagged, slots)


def row_of(ref, k, width):
    tiles = width // LANES
    return jnp.concatenate([ref[k * tiles + t : k * tiles + t + 1, :] for t in range(tiles)], axis=1)


def one_of(low):
    shape = WIDE, low.shape[1]
    row = lax.broadcasted_iota(jnp.int32, shape, 0)
    return jnp.where(row == jnp.broadcast_to(low, shape), 1.0, 0.0).astype(jnp.bfloat16)


def fetch_blocks(weight_ref, held, sems):
    return lambda k: pltpu.make_async_copy(weight_ref.at[k], held.at[k], sems.at[k])


def forward_kernel(
    ocean_ref, heat_ref, weight_ref, arrived_ref, slot_ref, mask_ref, flux_ref, out_ref, source_ref,
    held, total, sems,
):
    owners, fields, _ = arrived_ref.shape
    slots = slot_ref.shape[1]
    highs = total.shape[0] // fields
    fetch = fetch_blocks(weight_ref, held, sems)
    for k in range(owners):
        fetch(k).start()
    total[...] = jnp.zeros_like(total)
    zero = jnp.zeros((fields, slots), jnp.bfloat16)

    def added(k):
        value_high, value_low = split(arrived_ref[k])
        weight_high, weight_low = split(held[k])
        both = dot_nt(jnp.concatenate([value_high, value_low], axis=0), weight_high)
        mapped = (both[fields:] + dot_nt(value_high, weight_low)) + both[:fields]
        parts = split(mapped)
        cell = slot_ref[pl.ds(k, 1), :]
        high = jnp.broadcast_to(cell >> 8, (fields, slots)).astype(jnp.float32)
        high = high.astype(jnp.bfloat16)
        spread = one_of(cell & (WIDE - 1))
        here = [high == jnp.bfloat16(h) for h in range(highs)]
        rows = [
            jnp.concatenate([jnp.where(here[h], part, zero) for h in range(highs)], axis=0)
            for part in parts
        ]
        return dot_nt(rows[1], spread) + dot_nt(rows[0], spread)

    def body(turn, carry):
        for k in range(GROUP):
            fetch(turn * GROUP + k).wait()
        parts = [added(turn * GROUP + k) for k in range(GROUP)]
        total[...] += functools.reduce(lambda a, b: a + b, parts)
        return carry

    lax.fori_loop(0, owners // GROUP, body, 0)
    ocean = ocean_ref[0]
    sub = lax.broadcasted_iota(jnp.int32, (fields, WIDE), 0)
    heat = jnp.zeros((fields, WIDE), jnp.float32)
    for f in range(fields):
        heat = jnp.where(sub == f, heat_ref[f], heat)
    for h in range(highs):
        cut = slice(h * WIDE, (h + 1) * WIDE)
        wet = row_of(mask_ref, h, WIDE).astype(jnp.float32)
        block = total[h * fields : (h + 1) * fields, :] * wet
        out_ref[:, cut] = jnp.where(ocean == 1, block, flux_ref[:, cut])
        source = jnp.sum(heat * block, axis=0, keepdims=True)
        source = jnp.where(ocean == 1, source, 0.0)
        for t in range(WIDE // LANES):
            at = h * (WIDE // LANES) + t
            source_ref[at : at + 1, :] = source[:, t * LANES : (t + 1) * LANES]


def forward(ocean, heating, weights, arrived, slots, mask, flux):
    owners, fields, _ = arrived.shape
    cells = flux.shape[1]
    return pl.pallas_call(
        forward_kernel,
        in_specs=[scalars()] * 2 + [anywhere()] + [whole()] * 4,
        out_specs=[whole()] * 2,
        out_shape=[
            jax.ShapeDtypeStruct((fields, cells), jnp.float32),
            jax.ShapeDtypeStruct((cells // LANES, LANES), jnp.float32),
        ],
        scratch_shapes=[
            pltpu.VMEM(weights.shape, jnp.float32),
            pltpu.VMEM((cells // WIDE * fields, WIDE), jnp.float32),
            pltpu.SemaphoreType.DMA((owners,)),
        ],
        compiler_params=params(),
        name="forward",
    )(ocean, heating, weights, arrived, slots, mask, flux)


def mix_source_kernel(before_ref, own_ref, after_ref, near_ref, edge_ref, _, out_ref):
    tiles = own_ref.shape[0]
    rim = before_ref.shape[0]
    neighbours = near_ref.shape[0]

    def tile_of(k):
        if k < rim:
            row = before_ref[k : k + 1, :]
        elif k < rim + tiles:
            row = own_ref[k - rim : k - rim + 1, :]
        else:
            row = after_ref[k - rim - tiles : k - rim - tiles + 1, :]
        return jnp.broadcast_to(row, (SUB, LANES))

    def body(group, carry):
        at = pl.ds(pl.multiple_of(group * SUB, SUB), SUB)
        keep = jnp.ones((SUB, LANES), jnp.float32)
        total = jnp.zeros((SUB, LANES), jnp.float32)
        for j in range(neighbours):
            edge = edge_ref[j, at, :]
            (found,) = pick_lanes(tiles + 2 * rim, [tile_of], near_ref[j, at, :])
            total = total + edge * found
            keep = keep - edge
        out_ref[at, :] = total + keep * own_ref[at, :]
        return carry

    lax.fori_loop(0, tiles // SUB, body, 0)


def mix_source(before, own, after, near, edges, wait):
    shape = near.shape[0], own.shape[0], LANES
    return pl.pallas_call(
        mix_source_kernel,
        in_specs=[whole()] * 5 + [anywhere()],
        out_specs=whole(),
        out_shape=jax.ShapeDtypeStruct(own.shape, jnp.float32),
        compiler_params=params(),
        name="mix_source",
    )(before, own, after, near.reshape(shape), edges.reshape(shape), wait)


def backward_kernel(
    ocean_ref, weight_ref, arrived_ref, slot_ref, surface_ref, out_ref, held, total, sems
):
    owners, slots = slot_ref.shape
    highs = total.shape[0]
    fetch = fetch_blocks(weight_ref, held, sems)
    for k in range(owners):
        fetch(k).start()
    total[...] = jnp.zeros_like(total)

    def added(k):
        weight_high, weight_low = split(held[k])
        value = arrived_ref[pl.ds(owners + k, 1), :]
        value = jnp.broadcast_to(value, (2 * SUB, value.shape[1]))
        value_high, value_low = split(value)
        mapped = (dot_nt(value_low, weight_high) + dot_nt(value_high, weight_low)) + dot_nt(
            value_high, weight_high
        )
        mapped = jnp.broadcast_to(mapped[:1], (highs, slots))
        cell = slot_ref[pl.ds(k, 1), :]
        high = jnp.broadcast_to(cell >> 8, (highs, slots))
        spread = one_of(cell & (WIDE - 1))
        here = lax.broadcasted_iota(jnp.int32, (highs, slots), 0) == high
        part_high, part_low = split(jnp.where(here, mapped, 0.0))
        return dot_nt(part_low, spread) + dot_nt(part_high, spread)

    def body(turn, carry):
        for k in range(GROUP):
            fetch(turn * GROUP + k).wait()
        parts = [added(turn * GROUP + k) for k in range(GROUP)]
        total[...] += functools.reduce(lambda a, b: a + b, parts)
        return carry

    lax.fori_loop(0, owners // GROUP, body, 0)
    for h in range(highs):
        row = jnp.where(ocean_ref[0] == 1, row_of(surface_ref, h, WIDE), total[h : h + 1, :])
        out_ref[:, h * WIDE : (h + 1) * WIDE] = row


def backward(ocean, weights, arrived, slots, surface):
    owners, _ = slots.shape
    cells = surface.shape[0] * LANES
    return pl.pallas_call(
        backward_kernel,
        in_specs=[scalars(), anywhere()] + [whole()] * 3,
        out_specs=whole(),
        out_shape=jax.ShapeDtypeStruct((1, cells), jnp.float32),
        scratch_shapes=[
            pltpu.VMEM(weights.shape, jnp.float32),
            pltpu.VMEM((cells // WIDE, WIDE), jnp.float32),
            pltpu.SemaphoreType.DMA((owners,)),
        ],
        compiler_params=params(),
        name="backward",
    )(ocean, weights, arrived, slots, surface)


def mixer(near_ref, edge_ref, table, factors, slots, near_sems, chunk_of, chunks):
    neighbours = near_ref.shape[0]

    def fetch(i, slot):
        start = pl.multiple_of(chunk_of(i) * CHUNK, CHUNK)
        return pltpu.make_async_copy(
            near_ref.at[:, :, pl.ds(start, CHUNK)], slots[slot], near_sems.at[slot]
        )

    def begin():
        for slot in range(BUFFERS - 1):
            fetch(slot, slot).start()

    def set_factors(i, half):
        cell = pl.multiple_of(chunk_of(i) * CHUNK, CHUNK)
        edges = [edge_ref[j, :, pl.ds(cell, CHUNK)] for j in range(neighbours)]
        keep = 1.0 - functools.reduce(lambda a, b: a + b, edges)
        rest = jnp.zeros((SUB - neighbours - 1, CHUNK), jnp.float32)
        factors[half] = jnp.concatenate(edges + [keep, rest], axis=0).T

    def run(ahead, emit):
        set_factors(0, 0)
        sub = lax.broadcasted_iota(jnp.int32, (SUB, LANES), 0)
        masks = [sub == s for s in range(SUB)]

        def body(turn, carry):
            for slot in range(BUFFERS):
                i = turn * BUFFERS + slot
                half = slot % 2
                fetch(i, slot).wait()

                @pl.when(i + BUFFERS - 1 < chunks)
                def _():
                    fetch(i + BUFFERS - 1, (slot + BUFFERS - 1) % BUFFERS).start()

                ahead(turn, slot, i)
                set_factors(jnp.minimum(i + 1, chunks - 1), 1 - half)
                cell = pl.multiple_of(chunk_of(i) * CHUNK, CHUNK)
                for g in range(CHUNK // SUB):
                    own = table[pl.ds(pl.multiple_of(HALO + cell + g * SUB, SUB), SUB), :]
                    part = factors[half, g * SUB : (g + 1) * SUB, :]
                    total = own * jnp.broadcast_to(
                        part[:, neighbours : neighbours + 1], (SUB, LANES)
                    )
                    for j in range(neighbours):
                        picked = None
                        for s in range(SUB):
                            where = slots[slot][j, 0, g * SUB + s]
                            row = jnp.broadcast_to(table[pl.ds(where, 1), :], (SUB, LANES))
                            picked = row if s == 0 else jnp.where(masks[s], row, picked)
                        total = total + jnp.broadcast_to(part[:, j : j + 1], (SUB, LANES)) * picked
                    emit(i, half, g * SUB, total)
            return carry

        lax.fori_loop(0, chunks // BUFFERS, body, 0)

    return begin, run


def run_rows(run, chunks, rows, out_ref, out_sems):
    length = BUFFERS * CHUNK
    turns = chunks // BUFFERS

    def copy(turn):
        at = pl.ds(pl.multiple_of(turn * length, length), length)
        return pltpu.make_async_copy(rows.at[at], out_ref.at[at], out_sems.at[turn])

    def ahead(turn, slot, i):
        if slot == 1:

            @pl.when(turn > 0)
            def _():
                copy(turn - 1).start()

    def emit(i, half, start, total):
        rows[pl.ds(pl.multiple_of(i * CHUNK + start, SUB), SUB), :] = total

    run(ahead, emit)
    copy(turns - 1).start()
    for turn in range(turns):
        copy(turn).wait()


def run_solve(run, chunks, solver_ref, mixed, levels, out_ref, out_sems):
    length = BUFFERS * CHUNK
    turns = chunks // BUFFERS

    def copy(turn):
        at = pl.ds(pl.multiple_of(turn * length, length), length)
        return pltpu.make_async_copy(levels.at[:, at], out_ref.at[:, at], out_sems.at[turn])

    def solve(i, half):
        high, low = split(mixed[half])
        solver_high, solver_low = split(solver_ref[...])
        levels[:, pl.ds(pl.multiple_of(i * CHUNK, CHUNK), CHUNK)] = (
            dot_nt(solver_high, low) + dot_nt(solver_low, high)
        ) + dot_nt(solver_high, high)

    def ahead(turn, slot, i):
        if slot == 1:

            @pl.when(turn > 0)
            def _():
                copy(turn - 1).start()

        solve(jnp.maximum(i - 1, 0), 1 - slot % 2)

    def emit(i, half, start, total):
        mixed[half, start : start + SUB, :] = total

    mixed[...] = jnp.zeros_like(mixed)
    run(ahead, emit)
    solve(chunks - 1, (chunks - 1) % 2)
    copy(turns - 1).start()
    for turn in range(turns):
        copy(turn).wait()


def mixer_scratch(rows, neighbours, turns):
    return [
        pltpu.VMEM((rows, LANES), jnp.float32),
        pltpu.VMEM((2, CHUNK, SUB), jnp.float32),
        *[pltpu.SMEM((neighbours, 1, CHUNK), jnp.int32)] * BUFFERS,
        pltpu.SemaphoreType.DMA((BUFFERS,)),
        pltpu.SemaphoreType.DMA((turns,)),
    ]


def rims_kernel(chunk_of, chunks, *refs):
    state_ref, before_ref, after_ref, near_ref, edge_ref, *refs = refs
    out_ref, table_ref, *refs = refs
    table, factors, *slots, near_sems, out_sems, field, rows, load_sems, table_sem = refs
    levels, cells = state_ref.shape
    places = [(before_ref, 0, HALO), (state_ref, HALO, cells), (after_ref, HALO + cells, HALO)]
    loads = [
        pltpu.make_async_copy(ref, field.at[:, pl.ds(start, length)], load_sems.at[k])
        for k, (ref, start, length) in enumerate(places)
    ]
    begin, run = mixer(near_ref, edge_ref, table, factors, slots, near_sems, chunk_of, chunks)
    for load in loads:
        load.start()
    begin()
    for load in loads:
        load.wait()
    rest = jnp.zeros((LANES - levels, LANES), jnp.float32)

    def turn_tiles(k, carry):
        width = SUB * LANES
        start = pl.multiple_of(k * width, width)
        block = field[:, pl.ds(start, width)]
        for t in range(SUB):
            tile = jnp.concatenate([block[:, t * LANES : (t + 1) * LANES], rest], axis=0)
            table[pl.ds(pl.multiple_of(start + t * LANES, LANES), LANES), :] = tile.T
        return carry

    lax.fori_loop(0, table.shape[0] // (SUB * LANES), turn_tiles, 0)
    save = pltpu.make_async_copy(table, table_ref, table_sem)
    save.start()
    run_rows(run, chunks, rows, out_ref, out_sems)
    save.wait()


def mix_rims(state, before, after, near, edges, chunk_of, chunks):
    levels, cells = state.shape
    extended = cells + 2 * HALO
    return pl.pallas_call(
        functools.partial(rims_kernel, chunk_of, chunks),
        in_specs=[anywhere()] * 4 + [whole()],
        out_specs=[anywhere(), anywhere()],
        out_shape=[
            jax.ShapeDtypeStruct((chunks * CHUNK, LANES), jnp.float32),
            jax.ShapeDtypeStruct((extended, LANES), jnp.float32),
        ],
        scratch_shapes=mixer_scratch(extended, near.shape[0], chunks // BUFFERS)
        + [
            pltpu.VMEM((levels, extended), jnp.float32),
            pltpu.VMEM((chunks * CHUNK, LANES), jnp.float32),
            pltpu.SemaphoreType.DMA((3,)),
            pltpu.SemaphoreType.DMA,
        ],
        compiler_params=params(),
        name="mix_rims",
    )(state, before, after, near, edges)


def inside_kernel(chunk_of, chunks, *refs):
    table_ref, near_ref, edge_ref, _, out_ref, *refs = refs
    table, factors, *slots, near_sems, out_sems, rows, table_sem = refs
    load = pltpu.make_async_copy(table_ref, table, table_sem)
    load.start()
    begin, run = mixer(near_ref, edge_ref, table, factors, slots, near_sems, chunk_of, chunks)
    begin()
    load.wait()
    run_rows(run, chunks, rows, out_ref, out_sems)


def mix_inside(table, near, edges, wait, chunk_of, chunks):
    return pl.pallas_call(
        functools.partial(inside_kernel, chunk_of, chunks),
        in_specs=[anywhere()] * 2 + [whole(), anywhere()],
        out_specs=anywhere(),
        out_shape=jax.ShapeDtypeStruct((chunks * CHUNK, LANES), jnp.float32),
        scratch_shapes=mixer_scratch(table.shape[0], near.shape[0], chunks // BUFFERS)
        + [pltpu.VMEM((chunks * CHUNK, LANES), jnp.float32), pltpu.SemaphoreType.DMA],
        compiler_params=params(),
        name="mix_inside",
    )(table, near, edges, wait)


def solve_kernel(pieces, *refs):
    piece_refs, refs = refs[: len(pieces)], refs[len(pieces) :]
    solver_ref, before_ref, own_ref, after_ref, mask_ref, slot_ref, near_ref, edge_ref, *refs = refs
    out_ref, surface_ref, payload_ref, *refs = refs
    table, factors, *slots, near_sems, out_sems, mixed, levels, piece_sems = refs
    chunks = out_ref.shape[1] // CHUNK
    tiles = own_ref.shape[0]
    loads = [
        pltpu.make_async_copy(
            ref.at[pl.ds(row, length)], table.at[pl.ds(start, length)], piece_sems.at[k]
        )
        for k, (ref, (row, start, length)) in enumerate(zip(piece_refs, pieces))
    ]
    for load in loads:
        load.start()
    begin, run = mixer(near_ref, edge_ref, table, factors, slots, near_sems, lambda i: i, chunks)
    begin()
    for load in loads:
        load.wait()
    lane = lax.broadcasted_iota(jnp.int32, (LANES, LANES), 1)

    def add_source(source_ref, first, start):
        columns = source_ref[pl.ds(first, SUB), :].T
        for t in range(SUB):
            at = pl.ds(pl.multiple_of(start + t * LANES, LANES), LANES)
            column = jnp.broadcast_to(columns[:, t : t + 1], (LANES, LANES))
            table[at, :] = table[at, :] + jnp.where(lane == 0, column, 0.0)

    def add_own(k, carry):
        first = pl.multiple_of(k * SUB, SUB)
        add_source(own_ref, first, HALO + first * LANES)
        return carry

    add_source(before_ref, 0, 0)
    lax.fori_loop(0, tiles // SUB, add_own, 0)
    add_source(after_ref, 0, HALO + tiles * LANES)
    run_solve(run, chunks, solver_ref, mixed, levels, out_ref, out_sems)

    for k in range(tiles):
        wet = mask_ref[k : k + 1, :].astype(jnp.float32)
        surface_ref[k : k + 1, :] = levels[:1, k * LANES : (k + 1) * LANES] * wet
    owners, slots = slot_ref.shape
    payload_ref[owners:, :] = jnp.zeros((owners, slots), jnp.float32)

    def surface_tile(k):
        return jnp.broadcast_to(surface_ref[k : k + 1, :], (SUB, LANES))

    def pick(group, carry):
        at = pl.ds(pl.multiple_of(group * SUB, SUB), SUB)
        for k in range(slots // LANES):
            cut = slice(k * LANES, (k + 1) * LANES)
            (found,) = pick_lanes(tiles, [surface_tile], slot_ref[at, cut])
            payload_ref[at, cut] = found
        return carry

    lax.fori_loop(0, owners // SUB, pick, 0)


def mix_solve(pieces, solver, before, own, after, mask, slots, near, edges):
    rows = sum(length for _, _, _, length in pieces)
    cells = own.shape[0] * LANES
    owners, count = slots.shape
    return pl.pallas_call(
        functools.partial(solve_kernel, [(row, start, length) for _, row, start, length in pieces]),
        in_specs=[anywhere()] * len(pieces)
        + [whole()] * 6
        + [anywhere(), whole()],
        out_specs=[anywhere(), whole(), whole()],
        out_shape=[
            jax.ShapeDtypeStruct((solver.shape[0], cells), jnp.float32),
            jax.ShapeDtypeStruct(own.shape, jnp.float32),
            jax.ShapeDtypeStruct((2 * owners, count), jnp.float32),
        ],
        scratch_shapes=mixer_scratch(rows, near.shape[0], cells // CHUNK // BUFFERS)
        + [
            pltpu.VMEM((2, CHUNK, LANES), jnp.float32),
            pltpu.VMEM((solver.shape[0], cells), jnp.float32),
            pltpu.SemaphoreType.DMA((len(pieces),)),
        ],
        compiler_params=params(),
        name="mix_solve",
    )(*[array for array, _, _, _ in pieces], solver, before, own, after, mask, slots, near, edges)


def to_neighbours(initial, last):
    count = lax.axis_size("blk")
    up = [(i, (i + 1) % count) for i in range(count)]
    down = [(j, i) for i, j in up]
    return lax.ppermute(last, "blk", up), lax.ppermute(initial, "blk", down)


def exchange(array, axes):
    return lax.all_to_all(array, axes, split_axis=0, concat_axis=0, tiled=True)


def shards(
    thermal_profiles,
    adjacent_positions,
    diffusion_link_factor,
    implicit_solver_matrix,
    lagged_surface_temp,
    flux_coefficient,
    flux_heating,
    ocean_cell_mask,
    atmosphere_slot_cells,
    ocean_slot_cells,
    forward_weight_blocks,
    backward_weight_blocks,
):
    ocean = lax.axis_index("comp").astype(jnp.int32).reshape(1)
    state = thermal_profiles[0]
    levels, cells = state.shape
    neighbours = adjacent_positions.shape[1]
    near = adjacent_positions.reshape(neighbours, 1, cells)
    edges = diffusion_link_factor.reshape(neighbours, 1, cells)
    mask = ocean_cell_mask.reshape(cells // LANES, LANES)
    atmosphere_slots = atmosphere_slot_cells[0]
    ocean_slots = ocean_slot_cells[0]
    solver = implicit_solver_matrix[0]
    twice = jnp.dot(solver, solver, precision=HIGHEST)
    twice = jnp.pad(twice, ((0, 0), (0, LANES - levels)))

    lowest = state[levels - 1 :]
    flux, payload = pack(
        ocean,
        flux_coefficient,
        lowest,
        lax.ppermute(lowest, "comp", [(0, 1)]),
        lagged_surface_temp.reshape(1, cells),
        atmosphere_slots,
    )
    arrived = exchange(payload, "blk")

    before, after = to_neighbours(state[:, :HALO], state[:, cells - HALO :])
    rim = HALO // CHUNK
    chunks = cells // CHUNK
    half = (chunks - 2 * rim) // 2
    rims, table = mix_rims(
        state,
        before,
        after,
        near,
        edges,
        lambda i: jnp.where(i < rim, i, i + chunks - 2 * rim),
        2 * rim,
    )
    next_before, next_after = to_neighbours(rims[:HALO], rims[HALO:])

    flux_out, source = forward(
        ocean,
        flux_heating,
        forward_weight_blocks[0],
        arrived,
        ocean_slots,
        mask,
        flux,
    )
    rim_rows = HALO // LANES
    source_before, source_after = to_neighbours(source[:rim_rows], source[-rim_rows:])
    low = mix_inside(table, near, edges, source, lambda i: i + rim, half)
    mixed = mix_source(source_before, source, source_after, near, edges, low)
    mixed_before, mixed_after = to_neighbours(mixed[:rim_rows], mixed[-rim_rows:])
    high = mix_inside(table, near, edges, mixed, lambda i: i + rim + half, half)

    middle = half * CHUNK
    result, surface, back_payload = mix_solve(
        [
            (next_before, 0, 0, HALO),
            (rims, 0, HALO, HALO),
            (low, 0, 2 * HALO, middle),
            (high, 0, 2 * HALO + middle, middle),
            (rims, HALO, 2 * HALO + 2 * middle, HALO),
            (next_after, 0, HALO + cells, HALO),
        ],
        twice,
        mixed_before,
        mixed,
        mixed_after,
        mask,
        ocean_slots,
        near,
        edges,
    )
    warmth = backward(
        ocean,
        backward_weight_blocks[0],
        exchange(back_payload, ("comp", "blk")),
        atmosphere_slots,
        surface,
    )
    return (result[None], flux_out[None], warmth)


def solution(mesh):
    placed = (
        P("comp", None, "blk"),
        P("comp", None, "blk"),
        P("comp", None, "blk"),
        P("comp", None, None),
        P("blk"),
        P(None, "blk"),
        P(),
        P("blk"),
        P("blk", None, None),
        P("blk", None, None),
        P("blk", None, None, None),
        P("blk", None, None, None),
    )
    return jax.shard_map(
        shards,
        mesh=mesh,
        in_specs=placed,
        out_specs=(P("comp", None, "blk"), P("comp", None, "blk"), P("comp", "blk")),
        check_vma=False,
    )
```

time: 713 us -> 178 us (0.25)
  local copies, waits for them, and re-layouts: 527 us -> 11.3 us
  Pallas kernels: 0 us -> 126 us
  other arithmetic: 89.2 us -> 0 us
  matrix products: 36.4 us -> 0.17 us
  waiting for transfers between devices: 33.1 us -> 0.86 us
  blocking collectives: 0 us -> 9.02 us
    gather x28 -> x0, local copies, waits for them, and re-layouts: 494 us -> none  [the longest x24 429 us: advance(): picked = jnp.take(extended, nearby[j], axis=1)]
    pallas_call x0 -> x8, Pallas kernels: none -> 126 us  [the longest x1 41.7 us: mix_solve(): pl.pallas_call(functools.partial(solve_kernel, [(row, start, length) for...]
    scatter-add x2 -> x0, other arithmetic: 68.5 us -> none  [add_rows(): return start.at[where].add(values)]
    dot_general x4 -> x1, matrix products: 36.4 us -> 0.17 us  [shards(): twice = jnp.dot(solver, solver, precision=HIGHEST)]
    ppermute x4 -> x9, waiting for transfers between devices: 20.5 us -> 0.86 us  [the longest x1 0.84 us: shards(): lax.ppermute(lowest, 'comp', [(0, 1)])]
    ppermute x4 -> x9, starting transfers between devices: 11.3 us -> 25.4 us  [the longest x8 24 us: to_neighbours(): return (lax.ppermute(last, 'blk', up), lax.ppermute(initial, 'blk', down))]
    all_to_all x2 -> x1, waiting for transfers between devices: 12.6 us -> 0.01 us  [exchange(): return lax.all_to_all(array, axes, split_axis=0, concat_axis=0, tiled=True)]
    concatenate x3 -> x0, local copies, waits for them, and re-layouts: 9.37 us -> none  [the longest x2 9.36 us: with_halo(): shard = jnp.concatenate([before, shard, after], axis=dim)]
  transfers between devices with their start and end apart: 6 -> 10, of which waited for: 6 -> 1; matrix products, arithmetic and copies ran while one was open for 2% -> 2% of each run, Pallas kernels for 0% -> 42%
where the time goes in v2:
time: 178 us; the launch traced here: 177 us
  Pallas kernels  126 us (71%)
  starting transfers between devices  29 us (16%)
  local copies, waits for them, and re-layouts  11.3 us (6%)
  blocking collectives  9.02 us (5%)
    pallas_call x1, Pallas kernels, mix_solve(): pl.pallas_call(functools.partial(solve_kernel, [(row, start, length) for...  41.7 us
    pallas_call x2, Pallas kernels, mix_inside(): pl.pallas_call(functools.partial(inside_kernel, chunk_of, chunks), in_spe...  32.5 us
    ppermute x8, starting transfers between devices, to_neighbours(): return (lax.ppermute(last, 'blk', up), lax.ppermute(initial, 'blk', down))  24 us
    pallas_call x1, Pallas kernels, forward(): pl.pallas_call(forward_kernel, in_specs=[scalars()] * 2 + [anywhere()] +...  15.4 us
    pallas_call x1, Pallas kernels, mix_rims(): pl.pallas_call(functools.partial(rims_kernel, chunk_of, chunks), in_specs...  13.7 us
    all_to_all x1, blocking collectives, exchange(): return lax.all_to_all(array, axes, split_axis=0, concat_axis=0, tiled=True)  9.02 us
    pallas_call x1, Pallas kernels, backward(): pl.pallas_call(backward_kernel, in_specs=[scalars(), anywhere()] + [whole...  8.96 us
    pallas_call x1, Pallas kernels, pack(): pl.pallas_call(pack_kernel, in_specs=[scalars()] + [whole()] * 5, out_spe...  6.87 us
  transfers between devices with their start and end apart: 10, of which 1 were waited for; matrix products, arithmetic and copies ran while one was open for 2% of the time, Pallas kernels for 42%

profile of v2, /device:TPU:0, one launch (start us, length us, event | category | flops | bytes accessed | tf_op | source)
XLA Modules:
  0.0 177.0 jit_solution(3908002162120701741)
XLA Ops:
  0.6 0.0 copy-start
  0.6 1.1 fusion.2
  1.8 3.0 %collective-permute-start = (f32[80,1024]{1,0:T(8,128)S(1)}, f32[80,1024]{1,0:T(8,128)S(1)}, u32[]{:S(2)}, u32[]{:S(2)}) collective-permute-start(f32[80,1024]{1,0:T(8,128)S(1)} %get-tuple-element.22), channel_id=1, source_target_pairs={{0,1},{1,2},{2,3},{3,4},{4,5},{5,6},{6,7},{7,8},{8,9},{9,10},{10,1... | collective-permute-start | bytes 983048 | tf_op jit(solution)/shard_map/ppermute | solution.py:604
  4.8 4.1 %collective-permute-start.1 = (f32[80,1024]{1,0:T(8,128)S(1)}, f32[80,1024]{1,0:T(8,128)S(1)}, u32[]{:S(2)}, u32[]{:S(2)}) collective-permute-start(f32[80,1024]{1,0:T(8,128)S(1)} %get-tuple-element.21), channel_id=1, source_target_pairs={{1,0},{2,1},{3,2},{4,3},{5,4},{6,5},{7,6},{8,7},{9,8},{10,9},{11,1... | collective-permute-start | bytes 983048 | tf_op jit(solution)/shard_map/ppermute | solution.py:604
  8.8 1.0 slice_bitcast_fusion.own_ref
  9.8 0.0 copy-start.6
  9.8 1.5 collective-permute-start.3
  11.3 0.8 collective-permute-done.3.received_ref
  12.1 0.6 copy-done.7
  12.7 6.9 %pack.1 = (f32[16,8192]{1,0:T(8,128)}, f32[16,16,256]{2,1,0:T(8,128)}) custom-call(s32[1]{0:T(128)} %bitcast.3.ocean_ref, f32[16,8192]{1,0:T(8,128)} %coefficient_ref.1, f32[1,8192]{1,0:T(1,128)} %copy-done.6, f32[1,8192]{1,0:T(1,128)} %copy-done.7, f32[1,8192]{1,0:T(1,128)} %bitcast.45, s32[16,256]{1,0:T(8,128)} %bitcast.42), custom_call_target="tpu_custom_call" | custom-call | tf_op jit(solution)/shard_map/pack/pallas_call | solution.py:105
  19.6 3.5 %all-to-all-start = ((f32[16,16,256]{2,1,0:T(8,128)}), f32[16,16,256]{2,1,0:T(8,128)S(1)}, u32[]{:S(2)}, u32[]{:S(2)}) async-start(f32[16,16,256]{2,1,0:T(8,128)} %get-tuple-element.14), calls=%async_computation | async-start | bytes 524288 | tf_op jit(solution)/shard_map/all_to_all | solution.py:608
  23.2 0.0 collective-permute-done.refs_1_
  23.2 0.0 copy-start.4
  23.2 0.7 copy-done.4
  23.9 0.1 copy-done.5
  24.0 13.7 %mix_rims.1 = (f32[2048,128]{1,0:T(8,128)}, f32[10240,128]{1,0:T(8,128)}) custom-call(f32[80,8192]{1,0:T(8,128)} %bitcast.36, f32[80,1024]{1,0:T(8,128)} %copy-done.4, f32[80,1024]{1,0:T(8,128)} %copy-done.5, s32[6,1,8192]{2,1,0:T(1,128)} %bitcast.25, f32[6,1,8192]{2,1,0:T(1,128)} %bitcast.30), custom_call_target="tpu_custom_call" | custom-call | tf_op jit(solution)/shard_map/mix_rims/pallas_call | solution.py:472
  37.7 1.3 fusion.3
  39.0 1.9 %collective-permute-start.2 = (f32[1024,128]{1,0:T(8,128)S(1)}, f32[1024,128]{1,0:T(8,128)S(1)}, u32[]{:S(2)}, u32[]{:S(2)}) collective-permute-start(f32[1024,128]{1,0:T(8,128)S(1)} %get-tuple-element.24), channel_id=1, source_target_pairs={{0,1},{1,2},{2,3},{3,4},{4,5},{5,6},{6,7},{7,8},{8,9},{9,10},{10,1... | collective-permute-start | bytes 1572872 | tf_op jit(solution)/shard_map/ppermute | solution.py:604
  40.8 3.8 %collective-permute-start.6 = (f32[1024,128]{1,0:T(8,128)S(1)}, f32[1024,128]{1,0:T(8,128)S(1)}, u32[]{:S(2)}, u32[]{:S(2)}) collective-permute-start(f32[1024,128]{1,0:T(8,128)S(1)} %get-tuple-element.23), channel_id=1, source_target_pairs={{1,0},{2,1},{3,2},{4,3},{5,4},{6,5},{7,6},{8,7},{9,8},{10,9},{11,1... | collective-permute-start | bytes 1572872 | tf_op jit(solution)/shard_map/ppermute | solution.py:604
  44.7 0.0 all-to-all-done.arrived_ref
  44.7 0.7 copy-done.1
  45.4 15.4 %forward.1 = (f32[16,8192]{1,0:T(8,128)}, f32[64,128]{1,0:T(8,128)}) custom-call(s32[1]{0:T(128)} %bitcast.3.ocean_ref, f32[16]{0:T(128)} %heat_ref.1, f32[16,512,256]{2,1,0:T(8,128)} %bitcast.23, f32[16,16,256]{2,1,0:T(8,128)} %copy-done.1, s32[16,512]{1,0:T(8,128)} %bitcast.38, s32[64,128]{1,0:T(8,128)} %bitcast.40, f32[16,8192]{1,0:T(8,128)} %get-tuple-element.15.flux_ref), custom_call_target="tpu_custom_call" | custom-call | tf_op jit(solution)/shard_map/forward/pallas_call | solution.py:191
  60.8 0.7 fusion.5
  61.5 0.0 collective-permute-start.4
  61.5 5.6 %collective-permute-start.5 = (f32[8,128]{1,0:T(8,128)S(1)}, f32[8,128]{1,0:T(8,128)S(1)}, u32[]{:S(2)}, u32[]{:S(2)}) collective-permute-start(f32[8,128]{1,0:T(8,128)S(1)} %get-tuple-element.27), channel_id=1, source_target_pairs={{1,0},{2,1},{3,2},{4,3},{5,4},{6,5},{7,6},{8,7},{9,8},{10,9},{11,1... | collective-permute-start | bytes 12296 | tf_op jit(solution)/shard_map/ppermute | solution.py:604
  67.1 16.3 %mix_inside.2._.refs_2_ = f32[3072,128]{1,0:T(8,128)} custom-call(f32[10240,128]{1,0:T(8,128)} %get-tuple-element.13.refs_0_, s32[6,1,8192]{2,1,0:T(1,128)} %bitcast.26, f32[6,1,8192]{2,1,0:T(1,128)} %bitcast.31, f32[64,128]{1,0:T(8,128)} %get-tuple-element.16.refs_3_.own_ref), custom_call_target="tpu_custom_call" | custom-call | tf_op jit(solution)/shard_map/mix_inside/pallas_call | solution.py:504
  83.4 0.0 copy-start.8
  83.4 0.0 collective-permute-done.5.after_ref
  83.4 0.6 copy-done.8
  84.0 0.0 copy-done.9
  84.0 6.5 %mix_source.1.refs_3_.refs_8_ = f32[64,128]{1,0:T(8,128)} custom-call(f32[8,128]{1,0:T(8,128)} %copy-done.8, f32[64,128]{1,0:T(8,128)} %get-tuple-element.16.refs_3_.own_ref, f32[8,128]{1,0:T(8,128)} %copy-done.9, s32[6,64,128]{2,1,0:T(8,128)} %bitcast.27, f32[6,64,128]{2,1,0:T(8,128)} %bitcast.32, f32[3072,128]{1,0:T(8,128)} %mix_inside.2._.refs_2_), custom_call_target="tpu_custom_call" | custom-call | tf_op jit(solution)/shard_map/mix_source/pallas_call | solution.py:240
  90.5 0.7 fusion.4
  91.2 0.0 collective-permute-start.7
  91.2 5.6 %collective-permute-start.8 = (f32[8,128]{1,0:T(8,128)S(1)}, f32[8,128]{1,0:T(8,128)S(1)}, u32[]{:S(2)}, u32[]{:S(2)}) collective-permute-start(f32[8,128]{1,0:T(8,128)S(1)} %get-tuple-element.25), channel_id=1, source_target_pairs={{1,0},{2,1},{3,2},{4,3},{5,4},{6,5},{7,6},{8,7},{9,8},{10,9},{11,1... | collective-permute-start | bytes 12296 | tf_op jit(solution)/shard_map/ppermute | solution.py:604
  96.8 0.2 fusion
  97.0 0.6 pad.4.refs_6_
  97.6 16.3 %mix_inside.3.refs_3_ = f32[3072,128]{1,0:T(8,128)} custom-call(f32[10240,128]{1,0:T(8,128)} %get-tuple-element.13.refs_0_, s32[6,1,8192]{2,1,0:T(1,128)} %bitcast.28, f32[6,1,8192]{2,1,0:T(1,128)} %bitcast.33, f32[64,128]{1,0:T(8,128)} %mix_source.1.refs_3_.refs_8_), custom_call_target="tpu_custom_call" | custom-call | tf_op jit(solution)/shard_map/mix_inside/pallas_call | solution.py:504
  113.9 0.0 collective-permute-done.7.refs_7_
  113.9 0.0 copy-start.10
  113.9 0.5 copy-done.10
  114.5 0.0 copy-done.11
  114.5 0.3 copy-done.2
  114.7 0.8 copy-done.3
  115.5 41.7 %mix_solve.1 = (f32[80,8192]{1,0:T(8,128)}, f32[64,128]{1,0:T(8,128)}, f32[32,512]{1,0:T(8,128)}) custom-call(f32[1024,128]{1,0:T(8,128)} %copy-done.2, f32[2048,128]{1,0:T(8,128)} %get-tuple-element.12.refs_1_.refs_4_, f32[3072,128]{1,0:T(8,128)} %mix_inside.2._.refs_2_, f32[3072,128]{1,0:T(8,128)} %mix_inside.3.refs_3_, ...), custom_call_target="tpu_custom_call" | custom-call | tf_op jit(solution)/shard_map/mix_solve/pallas_call | solution.py:578
  157.3 0.9 copy.15
  158.2 9.0 %all_to_all.16 = f32[32,1,512]{2,1,0:T(1,128)S(1)} all-to-all(f32[32,1,512]{2,1,0:T(1,128)S(1)} %copy.15), channel_id=1, replica_groups=mesh['comp'=2,'blk'=16] {'comp','blk'}, dimensions={0} | all-to-all | bytes 131072 | tf_op jit(solution)/shard_map/all_to_all | solution.py:608
  167.2 0.6 copy.18
  167.8 9.0 %backward.1 = f32[1,8192]{1,0:T(1,128)} custom-call(s32[1]{0:T(128)} %bitcast.3.ocean_ref, f32[16,256,512]{2,1,0:T(8,128)} %bitcast.24, f32[32,512]{1,0:T(8,128)} %bitcast.37, s32[16,256]{1,0:T(8,128)} %bitcast.43, f32[64,128]{1,0:T(8,128)} %get-tuple-element.20.surface_ref), custom_call_target="tpu_custom_call" | custom-call | tf_op jit(solution)/shard_map/backward/pallas_call | solution.py:292
  (14 shorter events, 0.0 us)
Async XLA Ops:
  0.6 96.2 %copy-start = (f32[1,80,80]{2,1,0:T(8,128)S(1)}, f32[1,80,80]{2,1,0:T(8,128)}, u32[]{:S(2)}) copy-start(f32[1,80,80]{2,1,0:T(8,128)} %param.15) | copy-start | bytes 76804
  1.8 21.4 %collective-permute-start = (f32[80,1024]{1,0:T(8,128)S(1)}, f32[80,1024]{1,0:T(8,128)S(1)}, u32[]{:S(2)}, u32[]{:S(2)}) collective-permute-start(f32[80,1024]{1,0:T(8,128)S(1)} %get-tuple-element.22), channel_id=1, source_target_pairs={{0,1},{1,2},{2,3},{3,4},{4,5},{5,6},{6,7},{7,8},{8,9},{9,10},{10,1... | collective-permute-start | bytes 983048 | tf_op jit(solution)/shard_map/ppermute | solution.py:604
  4.8 18.4 %collective-permute-start.1 = (f32[80,1024]{1,0:T(8,128)S(1)}, f32[80,1024]{1,0:T(8,128)S(1)}, u32[]{:S(2)}, u32[]{:S(2)}) collective-permute-start(f32[80,1024]{1,0:T(8,128)S(1)} %get-tuple-element.21), channel_id=1, source_target_pairs={{1,0},{2,1},{3,2},{4,3},{5,4},{6,5},{7,6},{8,7},{9,8},{10,9},{11,1... | collective-permute-start | bytes 983048 | tf_op jit(solution)/shard_map/ppermute | solution.py:604
  9.8 2.3 %copy-start.6 = (f32[1,8192]{1,0:T(1,128)}, f32[1,8192]{1,0:T(1,128)S(1)}, u32[]{:S(2)}) copy-start(f32[1,8192]{1,0:T(1,128)S(1)} %slice_bitcast_fusion.own_ref) | copy-start | bytes 98308
  9.8 2.3 %collective-permute-start.3 = (f32[1,8192]{1,0:T(1,128)S(1)}, f32[1,8192]{1,0:T(1,128)S(1)}, u32[]{:S(2)}, u32[]{:S(2)}) collective-permute-start(f32[1,8192]{1,0:T(1,128)S(1)} %slice_bitcast_fusion.own_ref), channel_id=1, source_target_pairs={{0,16},{1,17},{2,18},{3,19},{4,20},{5,21},{6,22},{7,23},{8,24},{9,... | collective-permute-start | bytes 98312 | tf_op jit(solution)/shard_map/ppermute | solution.py:643
  12.1 0.6 copy-start.7
  19.6 25.0 %all-to-all-start = ((f32[16,16,256]{2,1,0:T(8,128)}), f32[16,16,256]{2,1,0:T(8,128)S(1)}, u32[]{:S(2)}, u32[]{:S(2)}) async-start(f32[16,16,256]{2,1,0:T(8,128)} %get-tuple-element.14), calls=%async_computation | async-start | bytes 524288 | tf_op jit(solution)/shard_map/all_to_all | solution.py:608
  23.2 0.7 copy-start.4
  23.2 0.8 copy-start.5
  39.0 74.9 %collective-permute-start.2 = (f32[1024,128]{1,0:T(8,128)S(1)}, f32[1024,128]{1,0:T(8,128)S(1)}, u32[]{:S(2)}, u32[]{:S(2)}) collective-permute-start(f32[1024,128]{1,0:T(8,128)S(1)} %get-tuple-element.24), channel_id=1, source_target_pairs={{0,1},{1,2},{2,3},{3,4},{4,5},{5,6},{6,7},{7,8},{8,9},{9,10},{10,1... | collective-permute-start | bytes 1572872 | tf_op jit(solution)/shard_map/ppermute | solution.py:604
  40.8 73.1 %collective-permute-start.6 = (f32[1024,128]{1,0:T(8,128)S(1)}, f32[1024,128]{1,0:T(8,128)S(1)}, u32[]{:S(2)}, u32[]{:S(2)}) collective-permute-start(f32[1024,128]{1,0:T(8,128)S(1)} %get-tuple-element.23), channel_id=1, source_target_pairs={{1,0},{2,1},{3,2},{4,3},{5,4},{6,5},{7,6},{8,7},{9,8},{10,9},{11,1... | collective-permute-start | bytes 1572872 | tf_op jit(solution)/shard_map/ppermute | solution.py:604
  44.7 0.7 copy-start.1
  61.5 21.9 %collective-permute-start.4 = (f32[8,128]{1,0:T(8,128)S(1)}, f32[8,128]{1,0:T(8,128)S(1)}, u32[]{:S(2)}, u32[]{:S(2)}) collective-permute-start(f32[8,128]{1,0:T(8,128)S(1)} %get-tuple-element.28), channel_id=1, source_target_pairs={{0,1},{1,2},{2,3},{3,4},{4,5},{5,6},{6,7},{7,8},{8,9},{9,10},{10,1... | collective-permute-start | bytes 12296 | tf_op jit(solution)/shard_map/ppermute | solution.py:604
  61.5 21.9 %collective-permute-start.5 = (f32[8,128]{1,0:T(8,128)S(1)}, f32[8,128]{1,0:T(8,128)S(1)}, u32[]{:S(2)}, u32[]{:S(2)}) collective-permute-start(f32[8,128]{1,0:T(8,128)S(1)} %get-tuple-element.27), channel_id=1, source_target_pairs={{1,0},{2,1},{3,2},{4,3},{5,4},{6,5},{7,6},{8,7},{9,8},{10,9},{11,1... | collective-permute-start | bytes 12296 | tf_op jit(solution)/shard_map/ppermute | solution.py:604
  83.4 0.6 copy-start.8
  83.4 0.6 copy-start.9
  91.2 22.7 %collective-permute-start.7 = (f32[8,128]{1,0:T(8,128)S(1)}, f32[8,128]{1,0:T(8,128)S(1)}, u32[]{:S(2)}, u32[]{:S(2)}) collective-permute-start(f32[8,128]{1,0:T(8,128)S(1)} %get-tuple-element.26), channel_id=1, source_target_pairs={{0,1},{1,2},{2,3},{3,4},{4,5},{5,6},{6,7},{7,8},{8,9},{9,10},{10,1... | collective-permute-start | bytes 12296 | tf_op jit(solution)/shard_map/ppermute | solution.py:604
  91.2 22.7 %collective-permute-start.8 = (f32[8,128]{1,0:T(8,128)S(1)}, f32[8,128]{1,0:T(8,128)S(1)}, u32[]{:S(2)}, u32[]{:S(2)}) collective-permute-start(f32[8,128]{1,0:T(8,128)S(1)} %get-tuple-element.25), channel_id=1, source_target_pairs={{1,0},{2,1},{3,2},{4,3},{5,4},{6,5},{7,6},{8,7},{9,8},{10,9},{11,1... | collective-permute-start | bytes 12296 | tf_op jit(solution)/shard_map/ppermute | solution.py:604
  113.9 0.6 copy-start.10
  113.9 0.6 copy-start.11
  113.9 0.8 copy-start.2
  114.7 0.8 copy-start.3

commit v3 on v2

--- a/solution.py
+++ b/solution.py
@@ -8,13 +8,12 @@
 from jax.sharding import PartitionSpec as P
 
 HALO = 1024
-CHUNK = 128
+CHUNK = 256
 LANES = 128
 WIDE = 256
 SUB = 8
 BUFFERS = 4
 GROUP = 4
-LIMIT = 56 * 2**20
 HIGHEST = lax.Precision.HIGHEST
 
 
@@ -31,8 +30,8 @@
     return lax.dot_general(a, b, (((1,), (1,)), ((), ())), preferred_element_type=jnp.float32)
 
 
-def params():
-    return pltpu.CompilerParams(vmem_limit_bytes=LIMIT)
+def params(mebibytes=8):
+    return pltpu.CompilerParams(vmem_limit_bytes=mebibytes * 2**20)
 
 
 def whole():
@@ -45,6 +44,18 @@
 
 def anywhere():
     return pl.BlockSpec(memory_space=pl.ANY)
+
+
+def outside():
+    return pl.BlockSpec(memory_space=pltpu.HBM)
+
+
+def far(array):
+    return pltpu.with_memory_space_constraint(array, pltpu.HBM)
+
+
+def near_by(array):
+    return pltpu.with_memory_space_constraint(array, pltpu.VMEM)
 
 
 def lanes_from(row, lane):
@@ -107,7 +118,7 @@
         in_specs=[scalars()] + [whole()] * 5,
         out_specs=[whole()] * 2,
         out_shape=[
-            jax.ShapeDtypeStruct((fields, cells), jnp.float32),
+            pltpu.VMEM((fields, cells), jnp.float32),
             jax.ShapeDtypeStruct((owners, fields, count), jnp.float32),
         ],
         compiler_params=params(),
@@ -124,10 +135,6 @@
     shape = WIDE, low.shape[1]
     row = lax.broadcasted_iota(jnp.int32, shape, 0)
     return jnp.where(row == jnp.broadcast_to(low, shape), 1.0, 0.0).astype(jnp.bfloat16)
-
-
-def fetch_blocks(weight_ref, held, sems):
-    return lambda k: pltpu.make_async_copy(weight_ref.at[k], held.at[k], sems.at[k])
 
 
 def forward_kernel(
@@ -137,7 +144,10 @@
     owners, fields, _ = arrived_ref.shape
     slots = slot_ref.shape[1]
     highs = total.shape[0] // fields
-    fetch = fetch_blocks(weight_ref, held, sems)
+
+    def fetch(k):
+        return pltpu.make_async_copy(weight_ref.at[k], held.at[k], sems.at[k])
+
     for k in range(owners):
         fetch(k).start()
     total[...] = jnp.zeros_like(total)
@@ -190,7 +200,7 @@
     cells = flux.shape[1]
     return pl.pallas_call(
         forward_kernel,
-        in_specs=[scalars()] * 2 + [anywhere()] + [whole()] * 4,
+        in_specs=[scalars()] * 2 + [outside()] + [whole()] * 4,
         out_specs=[whole()] * 2,
         out_shape=[
             jax.ShapeDtypeStruct((fields, cells), jnp.float32),
@@ -201,7 +211,7 @@
             pltpu.VMEM((cells // WIDE * fields, WIDE), jnp.float32),
             pltpu.SemaphoreType.DMA((owners,)),
         ],
-        compiler_params=params(),
+        compiler_params=params(24),
         name="forward",
     )(ocean, heating, weights, arrived, slots, mask, flux)
 
@@ -236,7 +246,6 @@
 
 
 def mix_source(before, own, after, near, edges, wait):
-    shape = near.shape[0], own.shape[0], LANES
     return pl.pallas_call(
         mix_source_kernel,
         in_specs=[whole()] * 5 + [anywhere()],
@@ -244,21 +253,18 @@
         out_shape=jax.ShapeDtypeStruct(own.shape, jnp.float32),
         compiler_params=params(),
         name="mix_source",
-    )(before, own, after, near.reshape(shape), edges.reshape(shape), wait)
+    )(before, own, after, near, edges, wait)
 
 
 def backward_kernel(
-    ocean_ref, weight_ref, arrived_ref, slot_ref, surface_ref, out_ref, held, total, sems
+    ocean_ref, weight_ref, arrived_ref, slot_ref, surface_ref, out_ref, total
 ):
     owners, slots = slot_ref.shape
     highs = total.shape[0]
-    fetch = fetch_blocks(weight_ref, held, sems)
-    for k in range(owners):
-        fetch(k).start()
     total[...] = jnp.zeros_like(total)
 
     def added(k):
-        weight_high, weight_low = split(held[k])
+        weight_high, weight_low = split(weight_ref[k])
         value = arrived_ref[pl.ds(owners + k, 1), :]
         value = jnp.broadcast_to(value, (2 * SUB, value.shape[1]))
         value_high, value_low = split(value)
@@ -274,8 +280,6 @@
         return dot_nt(part_low, spread) + dot_nt(part_high, spread)
 
     def body(turn, carry):
-        for k in range(GROUP):
-            fetch(turn * GROUP + k).wait()
         parts = [added(turn * GROUP + k) for k in range(GROUP)]
         total[...] += functools.reduce(lambda a, b: a + b, parts)
         return carry
@@ -291,13 +295,11 @@
     cells = surface.shape[0] * LANES
     return pl.pallas_call(
         backward_kernel,
-        in_specs=[scalars(), anywhere()] + [whole()] * 3,
+        in_specs=[scalars()] + [whole()] * 4,
         out_specs=whole(),
         out_shape=jax.ShapeDtypeStruct((1, cells), jnp.float32),
         scratch_shapes=[
-            pltpu.VMEM(weights.shape, jnp.float32),
             pltpu.VMEM((cells // WIDE, WIDE), jnp.float32),
-            pltpu.SemaphoreType.DMA((owners,)),
         ],
         compiler_params=params(),
         name="backward",
@@ -318,8 +320,13 @@
             fetch(slot, slot).start()
 
     def set_factors(i, half):
-        cell = pl.multiple_of(chunk_of(i) * CHUNK, CHUNK)
-        edges = [edge_ref[j, :, pl.ds(cell, CHUNK)] for j in range(neighbours)]
+        tiles = CHUNK // LANES
+        edges = [
+            jnp.concatenate(
+                [edge_ref[j, pl.ds(chunk_of(i) * tiles + t, 1), :] for t in range(tiles)], axis=1
+            )
+            for j in range(neighbours)
+        ]
         keep = 1.0 - functools.reduce(lambda a, b: a + b, edges)
         rest = jnp.zeros((SUB - neighbours - 1, CHUNK), jnp.float32)
         factors[half] = jnp.concatenate(edges + [keep, rest], axis=0).T
@@ -363,30 +370,6 @@
     return begin, run
 
 
-def run_rows(run, chunks, rows, out_ref, out_sems):
-    length = BUFFERS * CHUNK
-    turns = chunks // BUFFERS
-
-    def copy(turn):
-        at = pl.ds(pl.multiple_of(turn * length, length), length)
-        return pltpu.make_async_copy(rows.at[at], out_ref.at[at], out_sems.at[turn])
-
-    def ahead(turn, slot, i):
-        if slot == 1:
-
-            @pl.when(turn > 0)
-            def _():
-                copy(turn - 1).start()
-
-    def emit(i, half, start, total):
-        rows[pl.ds(pl.multiple_of(i * CHUNK + start, SUB), SUB), :] = total
-
-    run(ahead, emit)
-    copy(turns - 1).start()
-    for turn in range(turns):
-        copy(turn).wait()
-
-
 def run_solve(run, chunks, solver_ref, mixed, levels, out_ref, out_sems):
     length = BUFFERS * CHUNK
     turns = chunks // BUFFERS
@@ -422,26 +405,26 @@
         copy(turn).wait()
 
 
-def mixer_scratch(rows, neighbours, turns):
+def mixer_scratch(neighbours):
     return [
-        pltpu.VMEM((rows, LANES), jnp.float32),
         pltpu.VMEM((2, CHUNK, SUB), jnp.float32),
         *[pltpu.SMEM((neighbours, 1, CHUNK), jnp.int32)] * BUFFERS,
         pltpu.SemaphoreType.DMA((BUFFERS,)),
-        pltpu.SemaphoreType.DMA((turns,)),
     ]
 
 
 def rims_kernel(chunk_of, chunks, *refs):
-    state_ref, before_ref, after_ref, near_ref, edge_ref, *refs = refs
-    out_ref, table_ref, *refs = refs
-    table, factors, *slots, near_sems, out_sems, field, rows, load_sems, table_sem = refs
+    state_ref, before_ref, after_ref, near_ref, near_tiles_ref, edge_tiles_ref, *refs = refs
+    table_ref, rims_ref, near_out, edge_ref, *refs = refs
+    factors, *slots, near_sems, table, field, load_sems, table_sem = refs
     levels, cells = state_ref.shape
     places = [(before_ref, 0, HALO), (state_ref, HALO, cells), (after_ref, HALO + cells, HALO)]
     loads = [
         pltpu.make_async_copy(ref, field.at[:, pl.ds(start, length)], load_sems.at[k])
         for k, (ref, start, length) in enumerate(places)
     ]
+    loads.append(pltpu.make_async_copy(near_tiles_ref, near_out, load_sems.at[3]))
+    loads.append(pltpu.make_async_copy(edge_tiles_ref, edge_ref, load_sems.at[4]))
     begin, run = mixer(near_ref, edge_ref, table, factors, slots, near_sems, chunk_of, chunks)
     for load in loads:
         load.start()
@@ -462,76 +445,115 @@
     lax.fori_loop(0, table.shape[0] // (SUB * LANES), turn_tiles, 0)
     save = pltpu.make_async_copy(table, table_ref, table_sem)
     save.start()
-    run_rows(run, chunks, rows, out_ref, out_sems)
+
+    def emit(i, half, start, total):
+        rims_ref[pl.ds(pl.multiple_of(i * CHUNK + start, SUB), SUB), :] = total
+
+    run(lambda turn, slot, i: None, emit)
     save.wait()
 
 
-def mix_rims(state, before, after, near, edges, chunk_of, chunks):
+def mix_rims(state, before, after, near, near_tiles, edge_tiles, chunk_of, chunks):
     levels, cells = state.shape
     extended = cells + 2 * HALO
     return pl.pallas_call(
         functools.partial(rims_kernel, chunk_of, chunks),
-        in_specs=[anywhere()] * 4 + [whole()],
-        out_specs=[anywhere(), anywhere()],
+        in_specs=[outside()] + [anywhere()] * 2 + [outside()] * 3,
+        out_specs=[outside()] + [whole()] * 3,
         out_shape=[
+            pltpu.HBM((extended, LANES), jnp.float32),
             jax.ShapeDtypeStruct((chunks * CHUNK, LANES), jnp.float32),
-            jax.ShapeDtypeStruct((extended, LANES), jnp.float32),
+            pltpu.VMEM(near_tiles.shape, jnp.int32),
+            pltpu.VMEM(edge_tiles.shape, jnp.float32),
         ],
-        scratch_shapes=mixer_scratch(extended, near.shape[0], chunks // BUFFERS)
+        scratch_shapes=mixer_scratch(near.shape[0])
         + [
+            pltpu.VMEM((extended, LANES), jnp.float32),
             pltpu.VMEM((levels, extended), jnp.float32),
-            pltpu.VMEM((chunks * CHUNK, LANES), jnp.float32),
-            pltpu.SemaphoreType.DMA((3,)),
+            pltpu.SemaphoreType.DMA((5,)),
             pltpu.SemaphoreType.DMA,
         ],
-        compiler_params=params(),
+        compiler_params=params(16),
         name="mix_rims",
-    )(state, before, after, near, edges)
-
-
-def inside_kernel(chunk_of, chunks, *refs):
-    table_ref, near_ref, edge_ref, _, out_ref, *refs = refs
-    table, factors, *slots, near_sems, out_sems, rows, table_sem = refs
-    load = pltpu.make_async_copy(table_ref, table, table_sem)
-    load.start()
+    )(state, before, after, near, near_tiles, edge_tiles)
+
+
+def low_kernel(chunk_of, chunks, *refs):
+    table_ref, rims_ref, near_ref, edge_ref, _, table, next_table, *refs = refs
+    factors, *slots, near_sems, load_sems = refs
+    last = next_table.shape[0] - 2 * HALO
+    places = [
+        (table_ref, table),
+        (rims_ref.at[pl.ds(0, HALO)], next_table.at[pl.ds(HALO, HALO)]),
+        (rims_ref.at[pl.ds(HALO, HALO)], next_table.at[pl.ds(last, HALO)]),
+    ]
+    loads = [pltpu.make_async_copy(*place, load_sems.at[k]) for k, place in enumerate(places)]
+    for load in loads:
+        load.start()
     begin, run = mixer(near_ref, edge_ref, table, factors, slots, near_sems, chunk_of, chunks)
     begin()
-    load.wait()
-    run_rows(run, chunks, rows, out_ref, out_sems)
-
-
-def mix_inside(table, near, edges, wait, chunk_of, chunks):
+    for load in loads:
+        load.wait()
+
+    def emit(i, half, start, total):
+        cell = HALO + chunk_of(i) * CHUNK + start
+        next_table[pl.ds(pl.multiple_of(cell, SUB), SUB), :] = total
+
+    run(lambda turn, slot, i: None, emit)
+
+
+def mix_low(table, rims, near, edges, wait, chunk_of, chunks):
     return pl.pallas_call(
-        functools.partial(inside_kernel, chunk_of, chunks),
-        in_specs=[anywhere()] * 2 + [whole(), anywhere()],
-        out_specs=anywhere(),
-        out_shape=jax.ShapeDtypeStruct((chunks * CHUNK, LANES), jnp.float32),
-        scratch_shapes=mixer_scratch(table.shape[0], near.shape[0], chunks // BUFFERS)
-        + [pltpu.VMEM((chunks * CHUNK, LANES), jnp.float32), pltpu.SemaphoreType.DMA],
+        functools.partial(low_kernel, chunk_of, chunks),
+        in_specs=[outside(), anywhere(), outside(), whole(), anywhere()],
+        out_specs=[whole()] * 2,
+        out_shape=[pltpu.VMEM(table.shape, jnp.float32)] * 2,
+        scratch_shapes=mixer_scratch(near.shape[0]) + [pltpu.SemaphoreType.DMA((3,))],
         compiler_params=params(),
-        name="mix_inside",
-    )(table, near, edges, wait)
-
-
-def solve_kernel(pieces, *refs):
-    piece_refs, refs = refs[: len(pieces)], refs[len(pieces) :]
-    solver_ref, before_ref, own_ref, after_ref, mask_ref, slot_ref, near_ref, edge_ref, *refs = refs
-    out_ref, surface_ref, payload_ref, *refs = refs
-    table, factors, *slots, near_sems, out_sems, mixed, levels, piece_sems = refs
+        name="mix_low",
+    )(table, rims, near, edges, wait)
+
+
+def high_kernel(chunk_of, chunks, *refs):
+    table, _, near_ref, edge_ref, _, next_table, factors, *slots, near_sems = refs
+    begin, run = mixer(near_ref, edge_ref, table, factors, slots, near_sems, chunk_of, chunks)
+    begin()
+
+    def emit(i, half, start, total):
+        cell = HALO + chunk_of(i) * CHUNK + start
+        next_table[pl.ds(pl.multiple_of(cell, SUB), SUB), :] = total
+
+    run(lambda turn, slot, i: None, emit)
+
+
+def mix_high(table, next_table, near, edges, wait, chunk_of, chunks):
+    return pl.pallas_call(
+        functools.partial(high_kernel, chunk_of, chunks),
+        in_specs=[whole()] * 2 + [outside(), whole(), anywhere()],
+        out_specs=whole(),
+        out_shape=pltpu.VMEM(next_table.shape, jnp.float32),
+        input_output_aliases={1: 0},
+        scratch_shapes=mixer_scratch(near.shape[0]),
+        compiler_params=params(),
+        name="mix_high",
+    )(table, next_table, near, edges, wait)
+
+
+def solve_kernel(*refs):
+    _, start_ref, end_ref, solver_ref, before_ref, own_ref, after_ref, *refs = refs
+    mask_ref, slot_ref, near_ref, edge_ref, *refs = refs
+    table, out_ref, surface_ref, payload_ref, *refs = refs
+    factors, *slots, near_sems, out_sems, mixed, levels, halo_sems = refs
     chunks = out_ref.shape[1] // CHUNK
     tiles = own_ref.shape[0]
     loads = [
-        pltpu.make_async_copy(
-            ref.at[pl.ds(row, length)], table.at[pl.ds(start, length)], piece_sems.at[k]
-        )
-        for k, (ref, (row, start, length)) in enumerate(zip(piece_refs, pieces))
+        pltpu.make_async_copy(ref, table.at[pl.ds(start, HALO)], halo_sems.at[k])
+        for k, (ref, start) in enumerate([(start_ref, 0), (end_ref, HALO + tiles * LANES)])
     ]
     for load in loads:
         load.start()
     begin, run = mixer(near_ref, edge_ref, table, factors, slots, near_sems, lambda i: i, chunks)
     begin()
-    for load in loads:
-        load.wait()
     lane = lax.broadcasted_iota(jnp.int32, (LANES, LANES), 1)
 
     def add_source(source_ref, first, start):
@@ -546,8 +568,10 @@
         add_source(own_ref, first, HALO + first * LANES)
         return carry
 
+    lax.fori_loop(0, tiles // SUB, add_own, 0)
+    for load in loads:
+        load.wait()
     add_source(before_ref, 0, 0)
-    lax.fori_loop(0, tiles // SUB, add_own, 0)
     add_source(after_ref, 0, HALO + tiles * LANES)
     run_solve(run, chunks, solver_ref, mixed, levels, out_ref, out_sems)
 
@@ -571,30 +595,31 @@
     lax.fori_loop(0, owners // SUB, pick, 0)
 
 
-def mix_solve(pieces, solver, before, own, after, mask, slots, near, edges):
-    rows = sum(length for _, _, _, length in pieces)
+def mix_solve(table, start, end, solver, before, own, after, mask, slots, near, edges):
     cells = own.shape[0] * LANES
     owners, count = slots.shape
+    levels = solver.shape[0]
     return pl.pallas_call(
-        functools.partial(solve_kernel, [(row, start, length) for _, row, start, length in pieces]),
-        in_specs=[anywhere()] * len(pieces)
-        + [whole()] * 6
-        + [anywhere(), whole()],
-        out_specs=[anywhere(), whole(), whole()],
+        solve_kernel,
+        in_specs=[whole()] + [anywhere()] * 2 + [whole()] * 6 + [outside(), whole()],
+        out_specs=[whole(), anywhere(), whole(), whole()],
         out_shape=[
-            jax.ShapeDtypeStruct((solver.shape[0], cells), jnp.float32),
+            pltpu.VMEM(table.shape, jnp.float32),
+            jax.ShapeDtypeStruct((levels, cells), jnp.float32),
             jax.ShapeDtypeStruct(own.shape, jnp.float32),
             jax.ShapeDtypeStruct((2 * owners, count), jnp.float32),
         ],
-        scratch_shapes=mixer_scratch(rows, near.shape[0], cells // CHUNK // BUFFERS)
+        input_output_aliases={0: 0},
+        scratch_shapes=mixer_scratch(near.shape[0])
         + [
+            pltpu.SemaphoreType.DMA((cells // CHUNK // BUFFERS,)),
             pltpu.VMEM((2, CHUNK, LANES), jnp.float32),
-            pltpu.VMEM((solver.shape[0], cells), jnp.float32),
-            pltpu.SemaphoreType.DMA((len(pieces),)),
+            pltpu.VMEM((levels, cells), jnp.float32),
+            pltpu.SemaphoreType.DMA((2,)),
         ],
         compiler_params=params(),
         name="mix_solve",
-    )(*[array for array, _, _, _ in pieces], solver, before, own, after, mask, slots, near, edges)
+    )(table, start, end, solver, before, own, after, mask, slots, near, edges)
 
 
 def to_neighbours(initial, last):
@@ -626,11 +651,12 @@
     state = thermal_profiles[0]
     levels, cells = state.shape
     neighbours = adjacent_positions.shape[1]
-    near = adjacent_positions.reshape(neighbours, 1, cells)
-    edges = diffusion_link_factor.reshape(neighbours, 1, cells)
-    mask = ocean_cell_mask.reshape(cells // LANES, LANES)
+    near = far(adjacent_positions.reshape(neighbours, 1, cells))
+    tiles = cells // LANES
+    mask = ocean_cell_mask.reshape(tiles, LANES)
     atmosphere_slots = atmosphere_slot_cells[0]
     ocean_slots = ocean_slot_cells[0]
+    backward_weights = near_by(backward_weight_blocks[0])
     solver = implicit_solver_matrix[0]
     twice = jnp.dot(solver, solver, precision=HIGHEST)
     twice = jnp.pad(twice, ((0, 0), (0, LANES - levels)))
@@ -638,11 +664,11 @@
     lowest = state[levels - 1 :]
     flux, payload = pack(
         ocean,
-        flux_coefficient,
+        far(flux_coefficient),
         lowest,
         lax.ppermute(lowest, "comp", [(0, 1)]),
-        lagged_surface_temp.reshape(1, cells),
-        atmosphere_slots,
+        far(lagged_surface_temp.reshape(1, cells)),
+        far(atmosphere_slots),
     )
     arrived = exchange(payload, "blk")
 
@@ -650,12 +676,13 @@
     rim = HALO // CHUNK
     chunks = cells // CHUNK
     half = (chunks - 2 * rim) // 2
-    rims, table = mix_rims(
-        state,
+    table, rims, near_tiles, edges = mix_rims(
+        far(state),
         before,
         after,
         near,
-        edges,
+        far(adjacent_positions.reshape(neighbours, tiles, LANES)),
+        far(diffusion_link_factor.reshape(neighbours, tiles, LANES)),
         lambda i: jnp.where(i < rim, i, i + chunks - 2 * rim),
         2 * rim,
     )
@@ -664,7 +691,7 @@
     flux_out, source = forward(
         ocean,
         flux_heating,
-        forward_weight_blocks[0],
+        far(forward_weight_blocks[0]),
         arrived,
         ocean_slots,
         mask,
@@ -672,21 +699,16 @@
     )
     rim_rows = HALO // LANES
     source_before, source_after = to_neighbours(source[:rim_rows], source[-rim_rows:])
-    low = mix_inside(table, near, edges, source, lambda i: i + rim, half)
-    mixed = mix_source(source_before, source, source_after, near, edges, low)
+    table, next_table = mix_low(far(table), rims, near, edges, source, lambda i: i + rim, half)
+    mixed = mix_source(source_before, source, source_after, near_tiles, edges, next_table)
     mixed_before, mixed_after = to_neighbours(mixed[:rim_rows], mixed[-rim_rows:])
-    high = mix_inside(table, near, edges, mixed, lambda i: i + rim + half, half)
-
-    middle = half * CHUNK
-    result, surface, back_payload = mix_solve(
-        [
-            (next_before, 0, 0, HALO),
-            (rims, 0, HALO, HALO),
-            (low, 0, 2 * HALO, middle),
-            (high, 0, 2 * HALO + middle, middle),
-            (rims, HALO, 2 * HALO + 2 * middle, HALO),
-            (next_after, 0, HALO + cells, HALO),
-        ],
+    next_table = mix_high(
+        table, next_table, near, edges, mixed, lambda i: i + rim + half, half
+    )
+    _, result, surface, back_payload = mix_solve(
+        next_table,
+        next_before,
+        next_after,
         twice,
         mixed_before,
         mixed,
@@ -698,7 +720,7 @@
     )
     warmth = backward(
         ocean,
-        backward_weight_blocks[0],
+        backward_weights,
         exchange(back_payload, ("comp", "blk")),
         atmosphere_slots,
         surface,

time: 178 us -> 150 us (0.84)
  Pallas kernels: 126 us -> 107 us
  local copies, waits for them, and re-layouts: 11.3 us -> 3.31 us
    pallas_call x5, Pallas kernels: 98.6 us -> 83.2 us  [the longest x1 36 us: mix_solve(): pl.pallas_call(solve_kernel, in_specs=[whole()] + [anywhere()] * 2 + [who...]
    unnamed x25 -> x15, local copies, waits for them, and re-layouts: 4.99 us -> 0.05 us
    pallas_call x1, Pallas kernels: 13.7 us -> 11.7 us  [mix_rims(): pl.pallas_call(functools.partial(rims_kernel, chunk_of, chunks), in_specs...]
  transfers between devices with their start and end apart: 10 -> 10, of which waited for: 1 -> 1; matrix products, arithmetic and copies ran while one was open for 2% -> 1% of each run, Pallas kernels for 42% -> 43%
where the time goes in v3:
time: 150 us
  Pallas kernels  107 us (71%)
  starting transfers between devices  29 us (19%)
  blocking collectives  9.02 us (6%)
  local copies, waits for them, and re-layouts  3.31 us (2%)
    pallas_call x1, Pallas kernels, mix_solve(): pl.pallas_call(solve_kernel, in_specs=[whole()] + [anywhere()] * 2 + [who...  36 us
    ppermute x8, starting transfers between devices, to_neighbours(): return (lax.ppermute(last, 'blk', up), lax.ppermute(initial, 'blk', down))  24 us
    pallas_call x1, Pallas kernels, forward(): pl.pallas_call(forward_kernel, in_specs=[scalars()] * 2 + [outside()] + [...  14.6 us
    pallas_call x1, Pallas kernels, mix_low(): pl.pallas_call(functools.partial(low_kernel, chunk_of, chunks), in_specs=...  14 us
    pallas_call x1, Pallas kernels, mix_high(): pl.pallas_call(functools.partial(high_kernel, chunk_of, chunks), in_specs...  12.2 us
    pallas_call x1, Pallas kernels, mix_rims(): pl.pallas_call(functools.partial(rims_kernel, chunk_of, chunks), in_specs...  11.7 us
    all_to_all x1, blocking collectives, exchange(): return lax.all_to_all(array, axes, split_axis=0, concat_axis=0, tiled=True)  9.02 us
    pallas_call x1, Pallas kernels, pack(): pl.pallas_call(pack_kernel, in_specs=[scalars()] + [whole()] * 5, out_spe...  6.95 us
  transfers between devices with their start and end apart: 10, of which 1 were waited for; matrix products, arithmetic and copies ran while one was open for 1% of the time, Pallas kernels for 43%

profile of v3, /device:TPU:0, one launch (start us, length us, event | category | flops | bytes accessed | tf_op | source)
XLA Modules:
  0.0 150.0 jit_solution(4283271875319072957)
XLA Ops:
  0.6 0.0 copy-start
  0.6 0.0 copy-start.2
  0.7 0.0 copy-start.1
  0.7 0.0 copy-start.4
  0.7 1.1 fusion.2
  1.8 3.0 %collective-permute-start = (f32[80,1024]{1,0:T(8,128)S(1)}, f32[80,1024]{1,0:T(8,128)S(1)}, u32[]{:S(2)}, u32[]{:S(2)}) collective-permute-start(f32[80,1024]{1,0:T(8,128)S(1)} %get-tuple-element.30), channel_id=1, source_target_pairs={{0,1},{1,2},{2,3},{3,4},{4,5},{5,6},{6,7},{7,8},{8,9},{9,10},{10,1... | collective-permute-start | bytes 983048 | tf_op jit(solution)/shard_map/ppermute | solution.py:629
  4.8 4.1 %collective-permute-start.1 = (f32[80,1024]{1,0:T(8,128)S(1)}, f32[80,1024]{1,0:T(8,128)S(1)}, u32[]{:S(2)}, u32[]{:S(2)}) collective-permute-start(f32[80,1024]{1,0:T(8,128)S(1)} %get-tuple-element.29), channel_id=1, source_target_pairs={{1,0},{2,1},{3,2},{4,3},{5,4},{6,5},{7,6},{8,7},{9,8},{10,9},{11,1... | collective-permute-start | bytes 983048 | tf_op jit(solution)/shard_map/ppermute | solution.py:629
  8.9 1.0 slice_bitcast_fusion.own_ref
  9.9 1.5 collective-permute-start.2
  11.3 0.8 collective-permute-done.2.received_ref
  12.2 7.0 %pack.1 = (f32[16,8192]{1,0:T(8,128)S(1)}, f32[16,16,256]{2,1,0:T(8,128)}) custom-call(s32[1]{0:T(128)} %bitcast.4.ocean_ref, f32[16,8192]{1,0:T(8,128)} %coefficient_ref.1, f32[1,8192]{1,0:T(1,128)S(1)} %slice_bitcast_fusion.own_ref, f32[1,8192]{1,0:T(1,128)S(1)} %collective-permute-done.2.received_ref, f32[1,8192]{1,0:T(1,128)} %bitcast.42, s32[16,256]{1,0:T(8,128)} %bitcast.30), custom_call_target="tpu_custom_call" | custom-call | tf_op jit(solution)/shard_map/pack/pallas_call | solution.py:116
  19.1 3.5 %all-to-all-start = ((f32[16,16,256]{2,1,0:T(8,128)}), f32[16,16,256]{2,1,0:T(8,128)S(1)}, u32[]{:S(2)}, u32[]{:S(2)}) async-start(f32[16,16,256]{2,1,0:T(8,128)} %get-tuple-element.19), calls=%async_computation | async-start | bytes 524288 | tf_op jit(solution)/shard_map/all_to_all | solution.py:633
  22.7 0.0 collective-permute-done.refs_1_
  22.7 0.0 collective-permute-done.1.refs_2_
  22.7 11.7 %mix_rims.1 = (f32[10240,128]{1,0:T(8,128)}, f32[2048,128]{1,0:T(8,128)S(1)}, s32[6,64,128]{2,1,0:T(8,128)S(1)}, f32[6,64,128]{2,1,0:T(8,128)S(1)}) custom-call(f32[80,8192]{1,0:T(8,128)} %bitcast.40, f32[80,1024]{1,0:T(8,128)S(1)} %collective-permute-done.refs_1_, f32[80,1024]{1,0:T(8,128)S(1)} %collective-permute-done.1.refs_2_, s32[6,1,8192]{2,1,0:T(1,128)} %bitcast.34, ...), custom_call_target="tpu_custom_call" | custom-call | tf_op jit(solution)/shard_map/mix_rims/pallas_call | solution.py:459
  34.4 1.1 fusion.3
  35.4 1.8 %collective-permute-start.5 = (f32[1024,128]{1,0:T(8,128)}, f32[1024,128]{1,0:T(8,128)S(1)}, u32[]{:S(2)}, u32[]{:S(2)}) collective-permute-start(f32[1024,128]{1,0:T(8,128)} %get-tuple-element.32), channel_id=1, source_target_pairs={{0,1},{1,2},{2,3},{3,4},{4,5},{5,6},{6,7},{7,8},{8,9},{9,10},{10,1... | collective-permute-start | bytes 1572872 | tf_op jit(solution)/shard_map/ppermute | solution.py:629
  37.2 3.8 %collective-permute-start.6 = (f32[1024,128]{1,0:T(8,128)}, f32[1024,128]{1,0:T(8,128)S(1)}, u32[]{:S(2)}, u32[]{:S(2)}) collective-permute-start(f32[1024,128]{1,0:T(8,128)} %get-tuple-element.31), channel_id=1, source_target_pairs={{1,0},{2,1},{3,2},{4,3},{5,4},{6,5},{7,6},{8,7},{9,8},{10,9},{11,1... | collective-permute-start | bytes 1572872 | tf_op jit(solution)/shard_map/ppermute | solution.py:629
  41.1 0.0 all-to-all-done.arrived_ref
  41.1 0.0 copy-done.2
  41.1 0.0 copy-done.1
  41.1 0.0 copy-done.4
  41.1 14.6 %forward.1 = (f32[16,8192]{1,0:T(8,128)}, f32[64,128]{1,0:T(8,128)S(1)}) custom-call(s32[1]{0:T(128)} %bitcast.4.ocean_ref, f32[16]{0:T(128)S(1)} %copy-done.4, f32[16,512,256]{2,1,0:T(8,128)} %bitcast.33, f32[16,16,256]{2,1,0:T(8,128)S(1)} %all-to-all-done.arrived_ref, s32[16,512]{1,0:T(8,128)S(1)} %bitcast.26, s32[64,128]{1,0:T(8,128)S(1)} %bitcast.28, ...), custom_call_target="tpu_custom_call" | custom-call | tf_op jit(solution)/shard_map/forward/pallas_call | solution.py:201
  55.8 0.1 collective-permute-start.3
  55.8 5.6 %collective-permute-start.4 = (f32[8,128]{1,0:T(8,128)S(1)}, f32[8,128]{1,0:T(8,128)S(1)}, u32[]{:S(2)}, u32[]{:S(2)}) collective-permute-start(f32[8,128]{1,0:T(8,128)S(1)} %get-tuple-element.35), channel_id=1, source_target_pairs={{1,0},{2,1},{3,2},{4,3},{5,4},{6,5},{7,6},{8,7},{9,8},{10,9},{11,1... | collective-permute-start | bytes 12296 | tf_op jit(solution)/shard_map/ppermute | solution.py:629
  61.4 14.0 %mix_low.1 = (f32[10240,128]{1,0:T(8,128)S(1)}, f32[10240,128]{1,0:T(8,128)S(1)}) custom-call(f32[10240,128]{1,0:T(8,128)} %get-tuple-element.16.refs_0_, f32[2048,128]{1,0:T(8,128)S(1)} %get-tuple-element.17.refs_1_, s32[6,1,8192]{2,1,0:T(1,128)} %bitcast.36, f32[6,64,128]{2,1,0:T(8,128)S(1)} %get-tuple-element.18.refs_3_.edge_ref.refs_10_, ...), custom_call_target="tpu_custom_call" | custom-call | tf_op jit(solution)/shard_map/mix_low/pallas_call | solution.py:506
  75.4 0.0 collective-permute-done.3.before_ref
  75.4 0.0 collective-permute-done.4.after_ref
  75.4 4.9 %mix_source.1.refs_4_.refs_5_ = f32[64,128]{1,0:T(8,128)S(1)} custom-call(f32[8,128]{1,0:T(8,128)S(1)} %collective-permute-done.3.before_ref, f32[64,128]{1,0:T(8,128)S(1)} %get-tuple-element.21.refs_4_.own_ref, f32[8,128]{1,0:T(8,128)S(1)} %collective-permute-done.4.after_ref, s32[6,64,128]{2,1,0:T(8,128)S(1)} %get-tuple-element.24.near_ref, ...), custom_call_target="tpu_custom_call" | custom-call | tf_op jit(solution)/shard_map/mix_source/pallas_call | solution.py:249
  80.3 0.1 collective-permute-start.7
  80.4 5.6 %collective-permute-start.8 = (f32[8,128]{1,0:T(8,128)S(1)}, f32[8,128]{1,0:T(8,128)S(1)}, u32[]{:S(2)}, u32[]{:S(2)}) collective-permute-start(f32[8,128]{1,0:T(8,128)S(1)} %get-tuple-element.33), channel_id=1, source_target_pairs={{1,0},{2,1},{3,2},{4,3},{5,4},{6,5},{7,6},{8,7},{9,8},{10,9},{11,1... | collective-permute-start | bytes 12296 | tf_op jit(solution)/shard_map/ppermute | solution.py:629
  86.0 0.0 copy-done
  86.0 0.2 fusion
  86.2 0.0 slice-start
  86.2 0.0 slice-start.1
  86.2 12.2 %mix_high.1.refs_0_ = f32[10240,128]{1,0:T(8,128)S(1)} custom-call(f32[10240,128]{1,0:T(8,128)S(1)} %get-tuple-element.22.refs_0_, f32[10240,128]{1,0:T(8,128)S(1)} %get-tuple-element.23._.refs_1_, s32[6,1,8192]{2,1,0:T(1,128)} %bitcast.37, f32[6,64,128]{2,1,0:T(8,128)S(1)} %get-tuple-element.18.refs_3_.edge_ref.refs_10_, ...), custom_call_target="tpu_custom_call", output_to_operand_aliasing={{}: (1, {})} | custom-call | tf_op jit(solution)/shard_map/mix_high/pallas_call | solution.py:530
  98.4 0.0 copy-start.3
  98.4 0.0 collective-permute-done.7.refs_4_
  98.4 0.0 collective-permute-done.8.refs_6_
  98.4 0.0 collective-permute-done.5.refs_1_
  98.4 0.0 collective-permute-done.6.refs_2_
  98.4 36.0 %mix_solve.1 = (f32[10240,128]{1,0:T(8,128)S(1)}, f32[80,8192]{1,0:T(8,128)}, f32[64,128]{1,0:T(8,128)S(1)}, f32[32,512]{1,0:T(8,128)S(1)}) custom-call(f32[10240,128]{1,0:T(8,128)S(1)} %mix_high.1.refs_0_, f32[1024,128]{1,0:T(8,128)S(1)} %collective-permute-done.5.refs_1_, ...), custom_call_target="tpu_custom_call", output_to_operand_aliasing={{0}: (0, {})} | custom-call | tf_op jit(solution)/shard_map/mix_solve/pallas_call | solution.py:602
  134.4 0.1 copy.17
  134.5 9.0 %all_to_all.16 = f32[32,1,512]{2,1,0:T(1,128)S(1)} all-to-all(f32[32,1,512]{2,1,0:T(1,128)S(1)} %copy.17), channel_id=1, replica_groups=mesh['comp'=2,'blk'=16] {'comp','blk'}, dimensions={0} | all-to-all | bytes 131072 | tf_op jit(solution)/shard_map/all_to_all | solution.py:633
  143.5 0.0 slice-done
  143.5 0.0 slice-done.1
  143.5 0.0 copy-done.3
  143.5 6.4 %backward.1 = f32[1,8192]{1,0:T(1,128)} custom-call(s32[1]{0:T(128)} %bitcast.4.ocean_ref, f32[16,256,512]{2,1,0:T(8,128)S(1)} %bitcast.24, f32[32,512]{1,0:T(8,128)S(1)} %bitcast.25, s32[16,256]{1,0:T(8,128)S(1)} %bitcast.31, f32[64,128]{1,0:T(8,128)S(1)} %get-tuple-element.28.surface_ref), custom_call_target="tpu_custom_call" | custom-call | tf_op jit(solution)/shard_map/backward/pallas_call | solution.py:296
  (5 shorter events, 0.0 us)
Async XLA Ops:
  0.6 85.3 %copy-start = (f32[1,80,80]{2,1,0:T(8,128)S(1)}, f32[1,80,80]{2,1,0:T(8,128)}, u32[]{:S(2)}) copy-start(f32[1,80,80]{2,1,0:T(8,128)} %param.15) | copy-start | bytes 76804
  0.6 40.4 %copy-start.2 = (s32[8192]{0:T(1024)S(1)}, s32[8192]{0:T(1024)}, u32[]{:S(2)}) copy-start(s32[8192]{0:T(1024)} %param.19) | copy-start | bytes 98308
  0.7 40.4 %copy-start.1 = (s32[1,16,512]{2,1,0:T(8,128)S(1)}, s32[1,16,512]{2,1,0:T(8,128)}, u32[]{:S(2)}) copy-start(s32[1,16,512]{2,1,0:T(8,128)} %param.21) | copy-start | bytes 98308
  0.7 40.4 %copy-start.4 = (f32[16]{0:T(128)S(1)}, f32[16]{0:T(128)}, u32[]{:S(2)}) copy-start(f32[16]{0:T(128)} %heat_ref.1) | copy-start | bytes 196
  1.8 20.8 %collective-permute-start = (f32[80,1024]{1,0:T(8,128)S(1)}, f32[80,1024]{1,0:T(8,128)S(1)}, u32[]{:S(2)}, u32[]{:S(2)}) collective-permute-start(f32[80,1024]{1,0:T(8,128)S(1)} %get-tuple-element.30), channel_id=1, source_target_pairs={{0,1},{1,2},{2,3},{3,4},{4,5},{5,6},{6,7},{7,8},{8,9},{9,10},{10,1... | collective-permute-start | bytes 983048 | tf_op jit(solution)/shard_map/ppermute | solution.py:629
  4.8 17.9 %collective-permute-start.1 = (f32[80,1024]{1,0:T(8,128)S(1)}, f32[80,1024]{1,0:T(8,128)S(1)}, u32[]{:S(2)}, u32[]{:S(2)}) collective-permute-start(f32[80,1024]{1,0:T(8,128)S(1)} %get-tuple-element.29), channel_id=1, source_target_pairs={{1,0},{2,1},{3,2},{4,3},{5,4},{6,5},{7,6},{8,7},{9,8},{10,9},{11,1... | collective-permute-start | bytes 983048 | tf_op jit(solution)/shard_map/ppermute | solution.py:629
  9.9 2.3 %collective-permute-start.2 = (f32[1,8192]{1,0:T(1,128)S(1)}, f32[1,8192]{1,0:T(1,128)S(1)}, u32[]{:S(2)}, u32[]{:S(2)}) collective-permute-start(f32[1,8192]{1,0:T(1,128)S(1)} %slice_bitcast_fusion.own_ref), channel_id=1, source_target_pairs={{0,16},{1,17},{2,18},{3,19},{4,20},{5,21},{6,22},{7,23},{8,24},{9,... | collective-permute-start | bytes 98312 | tf_op jit(solution)/shard_map/ppermute | solution.py:669
  19.1 22.0 %all-to-all-start = ((f32[16,16,256]{2,1,0:T(8,128)}), f32[16,16,256]{2,1,0:T(8,128)S(1)}, u32[]{:S(2)}, u32[]{:S(2)}) async-start(f32[16,16,256]{2,1,0:T(8,128)} %get-tuple-element.19), calls=%async_computation | async-start | bytes 524288 | tf_op jit(solution)/shard_map/all_to_all | solution.py:633
  35.4 63.0 %collective-permute-start.5 = (f32[1024,128]{1,0:T(8,128)}, f32[1024,128]{1,0:T(8,128)S(1)}, u32[]{:S(2)}, u32[]{:S(2)}) collective-permute-start(f32[1024,128]{1,0:T(8,128)} %get-tuple-element.32), channel_id=1, source_target_pairs={{0,1},{1,2},{2,3},{3,4},{4,5},{5,6},{6,7},{7,8},{8,9},{9,10},{10,1... | collective-permute-start | bytes 1572872 | tf_op jit(solution)/shard_map/ppermute | solution.py:629
  37.2 61.2 %collective-permute-start.6 = (f32[1024,128]{1,0:T(8,128)}, f32[1024,128]{1,0:T(8,128)S(1)}, u32[]{:S(2)}, u32[]{:S(2)}) collective-permute-start(f32[1024,128]{1,0:T(8,128)} %get-tuple-element.31), channel_id=1, source_target_pairs={{1,0},{2,1},{3,2},{4,3},{5,4},{6,5},{7,6},{8,7},{9,8},{10,9},{11,1... | collective-permute-start | bytes 1572872 | tf_op jit(solution)/shard_map/ppermute | solution.py:629
  55.8 19.6 %collective-permute-start.3 = (f32[8,128]{1,0:T(8,128)S(1)}, f32[8,128]{1,0:T(8,128)S(1)}, u32[]{:S(2)}, u32[]{:S(2)}) collective-permute-start(f32[8,128]{1,0:T(8,128)S(1)} %get-tuple-element.36), channel_id=1, source_target_pairs={{0,1},{1,2},{2,3},{3,4},{4,5},{5,6},{6,7},{7,8},{8,9},{9,10},{10,1... | collective-permute-start | bytes 12296 | tf_op jit(solution)/shard_map/ppermute | solution.py:629
  55.8 19.6 %collective-permute-start.4 = (f32[8,128]{1,0:T(8,128)S(1)}, f32[8,128]{1,0:T(8,128)S(1)}, u32[]{:S(2)}, u32[]{:S(2)}) collective-permute-start(f32[8,128]{1,0:T(8,128)S(1)} %get-tuple-element.35), channel_id=1, source_target_pairs={{1,0},{2,1},{3,2},{4,3},{5,4},{6,5},{7,6},{8,7},{9,8},{10,9},{11,1... | collective-permute-start | bytes 12296 | tf_op jit(solution)/shard_map/ppermute | solution.py:629
  80.3 18.1 %collective-permute-start.7 = (f32[8,128]{1,0:T(8,128)S(1)}, f32[8,128]{1,0:T(8,128)S(1)}, u32[]{:S(2)}, u32[]{:S(2)}) collective-permute-start(f32[8,128]{1,0:T(8,128)S(1)} %get-tuple-element.34), channel_id=1, source_target_pairs={{0,1},{1,2},{2,3},{3,4},{4,5},{5,6},{6,7},{7,8},{8,9},{9,10},{10,1... | collective-permute-start | bytes 12296 | tf_op jit(solution)/shard_map/ppermute | solution.py:629
  80.4 18.0 %collective-permute-start.8 = (f32[8,128]{1,0:T(8,128)S(1)}, f32[8,128]{1,0:T(8,128)S(1)}, u32[]{:S(2)}, u32[]{:S(2)}) collective-permute-start(f32[8,128]{1,0:T(8,128)S(1)} %get-tuple-element.33), channel_id=1, source_target_pairs={{1,0},{2,1},{3,2},{4,3},{5,4},{6,5},{7,6},{8,7},{9,8},{10,9},{11,1... | collective-permute-start | bytes 12296 | tf_op jit(solution)/shard_map/ppermute | solution.py:629
  86.2 57.3 %slice-start = ((s8[8388608]{0:T(1024)(128)(4,1)}), s8[4194304]{0:T(1024)(128)(4,1)S(1)}, s32[]{:S(2)}) async-start(s8[8388608]{0:T(1024)(128)(4,1)} %bitcast.22), calls=%async_computation.2 | async-start | bytes 8388608
  86.2 57.3 %slice-start.1 = ((s8[8388608]{0:T(1024)(128)(4,1)}), s8[4194304]{0:T(1024)(128)(4,1)S(1)}, s32[]{:S(2)}) async-start(s8[8388608]{0:T(1024)(128)(4,1)} %bitcast.22), calls=%async_computation.3 | async-start | bytes 8388608
  98.4 45.1 %copy-start.3 = (s32[1,16,256]{2,1,0:T(8,128)S(1)}, s32[1,16,256]{2,1,0:T(8,128)}, u32[]{:S(2)}) copy-start(s32[1,16,256]{2,1,0:T(8,128)} %param.20) | copy-start | bytes 49156

commit v4 on v3

--- a/solution.py
+++ b/solution.py
@@ -133,8 +133,9 @@
 
 def one_of(low):
     shape = WIDE, low.shape[1]
-    row = lax.broadcasted_iota(jnp.int32, shape, 0)
-    return jnp.where(row == jnp.broadcast_to(low, shape), 1.0, 0.0).astype(jnp.bfloat16)
+    row = lax.broadcasted_iota(jnp.int32, shape, 0).astype(jnp.float32).astype(jnp.bfloat16)
+    low = jnp.broadcast_to(low.astype(jnp.float32).astype(jnp.bfloat16), shape)
+    return jnp.where(row == low, jnp.bfloat16(1.0), jnp.bfloat16(0.0))
 
 
 def forward_kernel(
@@ -546,33 +547,37 @@
     factors, *slots, near_sems, out_sems, mixed, levels, halo_sems = refs
     chunks = out_ref.shape[1] // CHUNK
     tiles = own_ref.shape[0]
-    loads = [
-        pltpu.make_async_copy(ref, table.at[pl.ds(start, HALO)], halo_sems.at[k])
-        for k, (ref, start) in enumerate([(start_ref, 0), (end_ref, HALO + tiles * LANES)])
-    ]
+    count = solver_ref.shape[0]
+    last = HALO + tiles * LANES
+    places = [(start_ref, table.at[pl.ds(0, HALO)]), (end_ref, table.at[pl.ds(last, HALO)])]
+    loads = [pltpu.make_async_copy(*place, halo_sems.at[k]) for k, place in enumerate(places)]
     for load in loads:
         load.start()
     begin, run = mixer(near_ref, edge_ref, table, factors, slots, near_sems, lambda i: i, chunks)
     begin()
     lane = lax.broadcasted_iota(jnp.int32, (LANES, LANES), 1)
 
-    def add_source(source_ref, first, start):
-        columns = source_ref[pl.ds(first, SUB), :].T
+    def add_source(source, start):
+        block = [
+            jnp.zeros((count, LANES), jnp.float32),
+            source,
+            jnp.zeros((LANES - count - SUB, LANES), jnp.float32),
+        ]
+        columns = jnp.concatenate(block, axis=0).T
         for t in range(SUB):
             at = pl.ds(pl.multiple_of(start + t * LANES, LANES), LANES)
-            column = jnp.broadcast_to(columns[:, t : t + 1], (LANES, LANES))
-            table[at, :] = table[at, :] + jnp.where(lane == 0, column, 0.0)
+            table[at, :] = table[at, :] + jnp.where(lane == count + t, columns, 0.0)
 
     def add_own(k, carry):
         first = pl.multiple_of(k * SUB, SUB)
-        add_source(own_ref, first, HALO + first * LANES)
+        add_source(own_ref[pl.ds(first, SUB), :], HALO + first * LANES)
         return carry
 
     lax.fori_loop(0, tiles // SUB, add_own, 0)
     for load in loads:
         load.wait()
-    add_source(before_ref, 0, 0)
-    add_source(after_ref, 0, HALO + tiles * LANES)
+    add_source(before_ref[...], 0)
+    add_source(after_ref[...], last)
     run_solve(run, chunks, solver_ref, mixed, levels, out_ref, out_sems)
 
     for k in range(tiles):
@@ -659,7 +664,14 @@
     backward_weights = near_by(backward_weight_blocks[0])
     solver = implicit_solver_matrix[0]
     twice = jnp.dot(solver, solver, precision=HIGHEST)
-    twice = jnp.pad(twice, ((0, 0), (0, LANES - levels)))
+    twice = jnp.concatenate(
+        [
+            twice,
+            jnp.broadcast_to(twice[:, :1], (levels, SUB)),
+            jnp.zeros((levels, LANES - levels - SUB), jnp.float32),
+        ],
+        axis=1,
+    )
 
     lowest = state[levels - 1 :]
     flux, payload = pack(
@@ -675,7 +687,7 @@
     before, after = to_neighbours(state[:, :HALO], state[:, cells - HALO :])
     rim = HALO // CHUNK
     chunks = cells // CHUNK
-    half = (chunks - 2 * rim) // 2
+    few = (chunks - 2 * rim) // 2
     table, rims, near_tiles, edges = mix_rims(
         far(state),
         before,
@@ -686,6 +698,7 @@
         lambda i: jnp.where(i < rim, i, i + chunks - 2 * rim),
         2 * rim,
     )
+
     next_before, next_after = to_neighbours(rims[:HALO], rims[HALO:])
 
     flux_out, source = forward(
@@ -699,11 +712,17 @@
     )
     rim_rows = HALO // LANES
     source_before, source_after = to_neighbours(source[:rim_rows], source[-rim_rows:])
-    table, next_table = mix_low(far(table), rims, near, edges, source, lambda i: i + rim, half)
+    table, next_table = mix_low(far(table), rims, near, edges, source, lambda i: i + rim, few)
     mixed = mix_source(source_before, source, source_after, near_tiles, edges, next_table)
     mixed_before, mixed_after = to_neighbours(mixed[:rim_rows], mixed[-rim_rows:])
     next_table = mix_high(
-        table, next_table, near, edges, mixed, lambda i: i + rim + half, half
+        table,
+        next_table,
+        near,
+        edges,
+        mixed,
+        lambda i: i + rim + few,
+        chunks - 2 * rim - few,
     )
     _, result, surface, back_payload = mix_solve(
         next_table,

time: 150 us -> 148 us (0.987)
  Pallas kernels: 107 us -> 104 us
    pallas_call x1, Pallas kernels: 36 us -> 33.9 us  [mix_solve(): pl.pallas_call(solve_kernel, in_specs=[whole()] + [anywhere()] * 2 + [who...]
  transfers between devices with their start and end apart: 10 -> 10, of which waited for: 1 -> 1; matrix products, arithmetic and copies ran while one was open for 1% -> 2% of each run, Pallas kernels for 43% -> 43%
where the time goes in v4:
time: 148 us
  Pallas kernels  104 us (70%)
  starting transfers between devices  29 us (20%)
  blocking collectives  9.02 us (6%)
  local copies, waits for them, and re-layouts  3.54 us (2%)
    pallas_call x1, Pallas kernels, mix_solve(): pl.pallas_call(solve_kernel, in_specs=[whole()] + [anywhere()] * 2 + [who...  33.9 us
    ppermute x8, starting transfers between devices, to_neighbours(): return (lax.ppermute(last, 'blk', up), lax.ppermute(initial, 'blk', down))  24 us
    pallas_call x1, Pallas kernels, forward(): pl.pallas_call(forward_kernel, in_specs=[scalars()] * 2 + [outside()] + [...  14.4 us
    pallas_call x1, Pallas kernels, mix_low(): pl.pallas_call(functools.partial(low_kernel, chunk_of, chunks), in_specs=...  14 us
    pallas_call x1, Pallas kernels, mix_high(): pl.pallas_call(functools.partial(high_kernel, chunk_of, chunks), in_specs...  12.2 us
    pallas_call x1, Pallas kernels, mix_rims(): pl.pallas_call(functools.partial(rims_kernel, chunk_of, chunks), in_specs...  11.7 us
    all_to_all x1, blocking collectives, exchange(): return lax.all_to_all(array, axes, split_axis=0, concat_axis=0, tiled=True)  9.02 us
    pallas_call x1, Pallas kernels, pack(): pl.pallas_call(pack_kernel, in_specs=[scalars()] + [whole()] * 5, out_spe...  6.95 us
  transfers between devices with their start and end apart: 10, of which 1 were waited for; matrix products, arithmetic and copies ran while one was open for 2% of the time, Pallas kernels for 43%

profile of v4, /device:TPU:0, one launch (start us, length us, event | category | flops | bytes accessed | tf_op | source)
XLA Modules:
  0.0 147.9 jit_solution(17169004055948350530)
XLA Ops:
  0.6 0.0 copy-start
  0.6 0.0 copy-start.2
  0.7 0.0 copy-start.1
  0.7 0.0 copy-start.4
  0.7 1.1 fusion.2
  1.8 3.0 %collective-permute-start = (f32[80,1024]{1,0:T(8,128)S(1)}, f32[80,1024]{1,0:T(8,128)S(1)}, u32[]{:S(2)}, u32[]{:S(2)}) collective-permute-start(f32[80,1024]{1,0:T(8,128)S(1)} %get-tuple-element.30), channel_id=1, source_target_pairs={{0,1},{1,2},{2,3},{3,4},{4,5},{5,6},{6,7},{7,8},{8,9},{9,10},{10,1... | collective-permute-start | bytes 983048 | tf_op jit(solution)/shard_map/ppermute | solution.py:634
  4.8 4.1 %collective-permute-start.1 = (f32[80,1024]{1,0:T(8,128)S(1)}, f32[80,1024]{1,0:T(8,128)S(1)}, u32[]{:S(2)}, u32[]{:S(2)}) collective-permute-start(f32[80,1024]{1,0:T(8,128)S(1)} %get-tuple-element.29), channel_id=1, source_target_pairs={{1,0},{2,1},{3,2},{4,3},{5,4},{6,5},{7,6},{8,7},{9,8},{10,9},{11,1... | collective-permute-start | bytes 983048 | tf_op jit(solution)/shard_map/ppermute | solution.py:634
  8.9 1.0 slice_bitcast_fusion.own_ref
  9.9 1.5 collective-permute-start.2
  11.3 0.8 collective-permute-done.2.received_ref
  12.2 7.0 %pack.1 = (f32[16,8192]{1,0:T(8,128)S(1)}, f32[16,16,256]{2,1,0:T(8,128)}) custom-call(s32[1]{0:T(128)} %bitcast.4.ocean_ref, f32[16,8192]{1,0:T(8,128)} %coefficient_ref.1, f32[1,8192]{1,0:T(1,128)S(1)} %slice_bitcast_fusion.own_ref, f32[1,8192]{1,0:T(1,128)S(1)} %collective-permute-done.2.received_ref, f32[1,8192]{1,0:T(1,128)} %bitcast.42, s32[16,256]{1,0:T(8,128)} %bitcast.30), custom_call_target="tpu_custom_call" | custom-call | tf_op jit(solution)/shard_map/pack/pallas_call | solution.py:116
  19.1 3.5 %all-to-all-start = ((f32[16,16,256]{2,1,0:T(8,128)}), f32[16,16,256]{2,1,0:T(8,128)S(1)}, u32[]{:S(2)}, u32[]{:S(2)}) async-start(f32[16,16,256]{2,1,0:T(8,128)} %get-tuple-element.19), calls=%async_computation | async-start | bytes 524288 | tf_op jit(solution)/shard_map/all_to_all | solution.py:638
  22.7 0.0 copy-done
  22.7 0.2 fusion
  22.8 0.0 collective-permute-done.refs_1_
  22.9 0.0 collective-permute-done.1.refs_2_
  22.9 11.7 %mix_rims.1 = (f32[10240,128]{1,0:T(8,128)}, f32[2048,128]{1,0:T(8,128)S(1)}, s32[6,64,128]{2,1,0:T(8,128)S(1)}, f32[6,64,128]{2,1,0:T(8,128)S(1)}) custom-call(f32[80,8192]{1,0:T(8,128)} %bitcast.40, f32[80,1024]{1,0:T(8,128)S(1)} %collective-permute-done.refs_1_, f32[80,1024]{1,0:T(8,128)S(1)} %collective-permute-done.1.refs_2_, s32[6,1,8192]{2,1,0:T(1,128)} %bitcast.34, ...), custom_call_target="tpu_custom_call" | custom-call | tf_op jit(solution)/shard_map/mix_rims/pallas_call | solution.py:460
  34.6 1.0 fusion.3
  35.6 1.8 %collective-permute-start.5 = (f32[1024,128]{1,0:T(8,128)}, f32[1024,128]{1,0:T(8,128)S(1)}, u32[]{:S(2)}, u32[]{:S(2)}) collective-permute-start(f32[1024,128]{1,0:T(8,128)} %get-tuple-element.32), channel_id=1, source_target_pairs={{0,1},{1,2},{2,3},{3,4},{4,5},{5,6},{6,7},{7,8},{8,9},{9,10},{10,1... | collective-permute-start | bytes 1572872 | tf_op jit(solution)/shard_map/ppermute | solution.py:634
  37.4 3.8 %collective-permute-start.6 = (f32[1024,128]{1,0:T(8,128)}, f32[1024,128]{1,0:T(8,128)S(1)}, u32[]{:S(2)}, u32[]{:S(2)}) collective-permute-start(f32[1024,128]{1,0:T(8,128)} %get-tuple-element.31), channel_id=1, source_target_pairs={{1,0},{2,1},{3,2},{4,3},{5,4},{6,5},{7,6},{8,7},{9,8},{10,9},{11,1... | collective-permute-start | bytes 1572872 | tf_op jit(solution)/shard_map/ppermute | solution.py:634
  41.2 0.0 all-to-all-done.arrived_ref
  41.2 0.0 copy-done.1
  41.2 0.0 copy-done.4
  41.3 14.4 %forward.1 = (f32[16,8192]{1,0:T(8,128)}, f32[64,128]{1,0:T(8,128)S(1)}) custom-call(s32[1]{0:T(128)} %bitcast.4.ocean_ref, f32[16]{0:T(128)S(1)} %copy-done.4, f32[16,512,256]{2,1,0:T(8,128)} %bitcast.33, f32[16,16,256]{2,1,0:T(8,128)S(1)} %all-to-all-done.arrived_ref, s32[16,512]{1,0:T(8,128)S(1)} %bitcast.26, s32[64,128]{1,0:T(8,128)S(1)} %bitcast.28, ...), custom_call_target="tpu_custom_call" | custom-call | tf_op jit(solution)/shard_map/forward/pallas_call | solution.py:202
  55.6 0.1 collective-permute-start.3
  55.7 5.6 %collective-permute-start.4 = (f32[8,128]{1,0:T(8,128)S(1)}, f32[8,128]{1,0:T(8,128)S(1)}, u32[]{:S(2)}, u32[]{:S(2)}) collective-permute-start(f32[8,128]{1,0:T(8,128)S(1)} %get-tuple-element.35), channel_id=1, source_target_pairs={{1,0},{2,1},{3,2},{4,3},{5,4},{6,5},{7,6},{8,7},{9,8},{10,9},{11,1... | collective-permute-start | bytes 12296 | tf_op jit(solution)/shard_map/ppermute | solution.py:634
  61.3 0.1 slice_reduce_fusion
  61.4 0.1 pad.2.clone
  61.5 14.0 %mix_low.1 = (f32[10240,128]{1,0:T(8,128)S(1)}, f32[10240,128]{1,0:T(8,128)S(1)}) custom-call(f32[10240,128]{1,0:T(8,128)} %get-tuple-element.16.refs_0_, f32[2048,128]{1,0:T(8,128)S(1)} %get-tuple-element.17.refs_1_, s32[6,1,8192]{2,1,0:T(1,128)} %bitcast.36, f32[6,64,128]{2,1,0:T(8,128)S(1)} %get-tuple-element.18.refs_3_.edge_ref.refs_10_, ...), custom_call_target="tpu_custom_call" | custom-call | tf_op jit(solution)/shard_map/mix_low/pallas_call | solution.py:507
  75.5 0.0 collective-permute-done.3.before_ref
  75.5 0.0 collective-permute-done.4.after_ref
  75.5 4.9 %mix_source.1.refs_4_.refs_5_ = f32[64,128]{1,0:T(8,128)S(1)} custom-call(f32[8,128]{1,0:T(8,128)S(1)} %collective-permute-done.3.before_ref, f32[64,128]{1,0:T(8,128)S(1)} %get-tuple-element.21.refs_4_.own_ref, f32[8,128]{1,0:T(8,128)S(1)} %collective-permute-done.4.after_ref, s32[6,64,128]{2,1,0:T(8,128)S(1)} %get-tuple-element.24.near_ref, ...), custom_call_target="tpu_custom_call" | custom-call | tf_op jit(solution)/shard_map/mix_source/pallas_call | solution.py:250
  80.4 0.1 collective-permute-start.7
  80.5 5.6 %collective-permute-start.8 = (f32[8,128]{1,0:T(8,128)S(1)}, f32[8,128]{1,0:T(8,128)S(1)}, u32[]{:S(2)}, u32[]{:S(2)}) collective-permute-start(f32[8,128]{1,0:T(8,128)S(1)} %get-tuple-element.33), channel_id=1, source_target_pairs={{1,0},{2,1},{3,2},{4,3},{5,4},{6,5},{7,6},{8,7},{9,8},{10,9},{11,1... | collective-permute-start | bytes 12296 | tf_op jit(solution)/shard_map/ppermute | solution.py:634
  86.1 0.1 broadcast_in_dim.17
  86.1 0.1 maximum_maximum_fusion.refs_3_
  86.2 0.0 slice-start
  86.2 0.0 slice-start.1
  86.2 12.2 %mix_high.1.refs_0_ = f32[10240,128]{1,0:T(8,128)S(1)} custom-call(f32[10240,128]{1,0:T(8,128)S(1)} %get-tuple-element.22.refs_0_, f32[10240,128]{1,0:T(8,128)S(1)} %get-tuple-element.23._.refs_1_, s32[6,1,8192]{2,1,0:T(1,128)} %bitcast.37, f32[6,64,128]{2,1,0:T(8,128)S(1)} %get-tuple-element.18.refs_3_.edge_ref.refs_10_, ...), custom_call_target="tpu_custom_call", output_to_operand_aliasing={{}: (1, {})} | custom-call | tf_op jit(solution)/shard_map/mix_high/pallas_call | solution.py:531
  98.4 0.0 copy-start.3
  98.4 0.0 collective-permute-done.7.refs_4_
  98.5 0.0 collective-permute-done.8.refs_6_
  98.5 0.0 collective-permute-done.5.refs_1_
  98.5 0.0 collective-permute-done.6.refs_2_
  98.5 33.9 %mix_solve.1 = (f32[10240,128]{1,0:T(8,128)S(1)}, f32[80,8192]{1,0:T(8,128)}, f32[64,128]{1,0:T(8,128)S(1)}, f32[32,512]{1,0:T(8,128)S(1)}) custom-call(f32[10240,128]{1,0:T(8,128)S(1)} %mix_high.1.refs_0_, f32[1024,128]{1,0:T(8,128)S(1)} %collective-permute-done.5.refs_1_, ...), custom_call_target="tpu_custom_call", output_to_operand_aliasing={{0}: (0, {})} | custom-call | tf_op jit(solution)/shard_map/mix_solve/pallas_call | solution.py:607
  132.3 0.1 copy.17
  132.4 9.0 %all_to_all.16 = f32[32,1,512]{2,1,0:T(1,128)S(1)} all-to-all(f32[32,1,512]{2,1,0:T(1,128)S(1)} %copy.17), channel_id=1, replica_groups=mesh['comp'=2,'blk'=16] {'comp','blk'}, dimensions={0} | all-to-all | bytes 131072 | tf_op jit(solution)/shard_map/all_to_all | solution.py:638
  141.5 6.4 %backward.1 = f32[1,8192]{1,0:T(1,128)} custom-call(s32[1]{0:T(128)} %bitcast.4.ocean_ref, f32[16,256,512]{2,1,0:T(8,128)S(1)} %bitcast.24, f32[32,512]{1,0:T(8,128)S(1)} %bitcast.25, s32[16,256]{1,0:T(8,128)S(1)} %bitcast.31, f32[64,128]{1,0:T(8,128)S(1)} %get-tuple-element.28.surface_ref), custom_call_target="tpu_custom_call" | custom-call | tf_op jit(solution)/shard_map/backward/pallas_call | solution.py:297
  (9 shorter events, 0.0 us)
Async XLA Ops:
  0.6 22.0 %copy-start = (f32[1,80,80]{2,1,0:T(8,128)S(1)}, f32[1,80,80]{2,1,0:T(8,128)}, u32[]{:S(2)}) copy-start(f32[1,80,80]{2,1,0:T(8,128)} %param.15) | copy-start | bytes 76804
  0.6 40.6 %copy-start.2 = (s32[8192]{0:T(1024)S(1)}, s32[8192]{0:T(1024)}, u32[]{:S(2)}) copy-start(s32[8192]{0:T(1024)} %param.19) | copy-start | bytes 98308
  0.7 40.6 %copy-start.1 = (s32[1,16,512]{2,1,0:T(8,128)S(1)}, s32[1,16,512]{2,1,0:T(8,128)}, u32[]{:S(2)}) copy-start(s32[1,16,512]{2,1,0:T(8,128)} %param.21) | copy-start | bytes 98308
  0.7 40.6 %copy-start.4 = (f32[16]{0:T(128)S(1)}, f32[16]{0:T(128)}, u32[]{:S(2)}) copy-start(f32[16]{0:T(128)} %heat_ref.1) | copy-start | bytes 196
  1.8 21.0 %collective-permute-start = (f32[80,1024]{1,0:T(8,128)S(1)}, f32[80,1024]{1,0:T(8,128)S(1)}, u32[]{:S(2)}, u32[]{:S(2)}) collective-permute-start(f32[80,1024]{1,0:T(8,128)S(1)} %get-tuple-element.30), channel_id=1, source_target_pairs={{0,1},{1,2},{2,3},{3,4},{4,5},{5,6},{6,7},{7,8},{8,9},{9,10},{10,1... | collective-permute-start | bytes 983048 | tf_op jit(solution)/shard_map/ppermute | solution.py:634
  4.8 18.0 %collective-permute-start.1 = (f32[80,1024]{1,0:T(8,128)S(1)}, f32[80,1024]{1,0:T(8,128)S(1)}, u32[]{:S(2)}, u32[]{:S(2)}) collective-permute-start(f32[80,1024]{1,0:T(8,128)S(1)} %get-tuple-element.29), channel_id=1, source_target_pairs={{1,0},{2,1},{3,2},{4,3},{5,4},{6,5},{7,6},{8,7},{9,8},{10,9},{11,1... | collective-permute-start | bytes 983048 | tf_op jit(solution)/shard_map/ppermute | solution.py:634
  9.9 2.3 %collective-permute-start.2 = (f32[1,8192]{1,0:T(1,128)S(1)}, f32[1,8192]{1,0:T(1,128)S(1)}, u32[]{:S(2)}, u32[]{:S(2)}) collective-permute-start(f32[1,8192]{1,0:T(1,128)S(1)} %slice_bitcast_fusion.own_ref), channel_id=1, source_target_pairs={{0,16},{1,17},{2,18},{3,19},{4,20},{5,21},{6,22},{7,23},{8,24},{9,... | collective-permute-start | bytes 98312 | tf_op jit(solution)/shard_map/ppermute | solution.py:681
  19.1 22.1 %all-to-all-start = ((f32[16,16,256]{2,1,0:T(8,128)}), f32[16,16,256]{2,1,0:T(8,128)S(1)}, u32[]{:S(2)}, u32[]{:S(2)}) async-start(f32[16,16,256]{2,1,0:T(8,128)} %get-tuple-element.19), calls=%async_computation | async-start | bytes 524288 | tf_op jit(solution)/shard_map/all_to_all | solution.py:638
  35.6 62.9 %collective-permute-start.5 = (f32[1024,128]{1,0:T(8,128)}, f32[1024,128]{1,0:T(8,128)S(1)}, u32[]{:S(2)}, u32[]{:S(2)}) collective-permute-start(f32[1024,128]{1,0:T(8,128)} %get-tuple-element.32), channel_id=1, source_target_pairs={{0,1},{1,2},{2,3},{3,4},{4,5},{5,6},{6,7},{7,8},{8,9},{9,10},{10,1... | collective-permute-start | bytes 1572872 | tf_op jit(solution)/shard_map/ppermute | solution.py:634
  37.4 61.1 %collective-permute-start.6 = (f32[1024,128]{1,0:T(8,128)}, f32[1024,128]{1,0:T(8,128)S(1)}, u32[]{:S(2)}, u32[]{:S(2)}) collective-permute-start(f32[1024,128]{1,0:T(8,128)} %get-tuple-element.31), channel_id=1, source_target_pairs={{1,0},{2,1},{3,2},{4,3},{5,4},{6,5},{7,6},{8,7},{9,8},{10,9},{11,1... | collective-permute-start | bytes 1572872 | tf_op jit(solution)/shard_map/ppermute | solution.py:634
  55.6 19.9 %collective-permute-start.3 = (f32[8,128]{1,0:T(8,128)S(1)}, f32[8,128]{1,0:T(8,128)S(1)}, u32[]{:S(2)}, u32[]{:S(2)}) collective-permute-start(f32[8,128]{1,0:T(8,128)S(1)} %get-tuple-element.36), channel_id=1, source_target_pairs={{0,1},{1,2},{2,3},{3,4},{4,5},{5,6},{6,7},{7,8},{8,9},{9,10},{10,1... | collective-permute-start | bytes 12296 | tf_op jit(solution)/shard_map/ppermute | solution.py:634
  55.7 19.8 %collective-permute-start.4 = (f32[8,128]{1,0:T(8,128)S(1)}, f32[8,128]{1,0:T(8,128)S(1)}, u32[]{:S(2)}, u32[]{:S(2)}) collective-permute-start(f32[8,128]{1,0:T(8,128)S(1)} %get-tuple-element.35), channel_id=1, source_target_pairs={{1,0},{2,1},{3,2},{4,3},{5,4},{6,5},{7,6},{8,7},{9,8},{10,9},{11,1... | collective-permute-start | bytes 12296 | tf_op jit(solution)/shard_map/ppermute | solution.py:634
  80.4 18.1 %collective-permute-start.7 = (f32[8,128]{1,0:T(8,128)S(1)}, f32[8,128]{1,0:T(8,128)S(1)}, u32[]{:S(2)}, u32[]{:S(2)}) collective-permute-start(f32[8,128]{1,0:T(8,128)S(1)} %get-tuple-element.34), channel_id=1, source_target_pairs={{0,1},{1,2},{2,3},{3,4},{4,5},{5,6},{6,7},{7,8},{8,9},{9,10},{10,1... | collective-permute-start | bytes 12296 | tf_op jit(solution)/shard_map/ppermute | solution.py:634
  80.5 18.0 %collective-permute-start.8 = (f32[8,128]{1,0:T(8,128)S(1)}, f32[8,128]{1,0:T(8,128)S(1)}, u32[]{:S(2)}, u32[]{:S(2)}) collective-permute-start(f32[8,128]{1,0:T(8,128)S(1)} %get-tuple-element.33), channel_id=1, source_target_pairs={{1,0},{2,1},{3,2},{4,3},{5,4},{6,5},{7,6},{8,7},{9,8},{10,9},{11,1... | collective-permute-start | bytes 12296 | tf_op jit(solution)/shard_map/ppermute | solution.py:634
  86.2 55.2 %slice-start = ((s8[8388608]{0:T(1024)(128)(4,1)}), s8[4194304]{0:T(1024)(128)(4,1)S(1)}, s32[]{:S(2)}) async-start(s8[8388608]{0:T(1024)(128)(4,1)} %bitcast.22), calls=%async_computation.2 | async-start | bytes 8388608
  86.2 55.2 %slice-start.1 = ((s8[8388608]{0:T(1024)(128)(4,1)}), s8[4194304]{0:T(1024)(128)(4,1)S(1)}, s32[]{:S(2)}) async-start(s8[8388608]{0:T(1024)(128)(4,1)} %bitcast.22), calls=%async_computation.3 | async-start | bytes 8388608
  98.4 43.0 %copy-start.3 = (s32[1,16,256]{2,1,0:T(8,128)S(1)}, s32[1,16,256]{2,1,0:T(8,128)}, u32[]{:S(2)}) copy-start(s32[1,16,256]{2,1,0:T(8,128)} %param.20) | copy-start | bytes 49156
